TPU v7x, 32 devices: a whole 2x2x4 slice. The times are simulated.
32 devices in a mesh: req: 4 (over z), vocab: 8 (over y, x, core).
Axes of the slice: x: 2, y: 2, z: 4, core: 2. Of those that a mesh axis runs over, the one named last changes fastest.
Arguments:
- hidden_states: bfloat16 [6144, 2048], P(('req', 'vocab')), may hold values from -400 to 400
- norm_gain: float32 [2048], replicated, may hold values from 0.25 to 1.75
- head_weight: bfloat16 [2048, 32000], P(None, 'vocab'), may hold values from -2 to 2
- targets: int32 [6144], P(('req', 'vocab')), may hold values from 0 to 31999
- lengths: int32 [256], P(('req', 'vocab')), may hold values from 1 to 24, as said below
- slot_of: int32 [256], P(('req', 'vocab')), may hold values from 0 to 255, each once
Outputs:
- logprob: float32 [256, 24], P(('req', 'vocab'))
- entropy: float32 [256, 24], P(('req', 'vocab'))
Inputs may be any that keep to these rules, and one draw needn't show every extreme that they name: The lengths of the 8 requests of one device sum to at most 128; some device's sum to exactly 128.
All inputs are finite; a program needn't handle non-finite values.
Results may differ from a plain program's by a relative error of at most 0.00097.
Values may be sent and summed in bfloat16 or wider, within the bound.
No kernel may reach another device: no remote copies, remote signals or barrier semaphores. Data moves between devices by JAX's collectives and lax.ppermute only.
A program may use at most 128 MiB of HBM per device.

v0:
```python
import jax
import jax.numpy as jnp
from jax import lax
from jax.sharding import PartitionSpec as P

eps_norm = 1e-05
block_rows = 512


def normalize(hidden_rows, norm_gain):
    values = hidden_rows.astype(jnp.float32)
    inverse_rms = lax.rsqrt(jnp.mean(values * values, axis=1, keepdims=True) + eps_norm)
    return (values * inverse_rms * norm_gain[None, :]).astype(jnp.bfloat16)


def piece_stats(piece_rows, piece_targets, head_weight, vocab_start):
    logits = jnp.dot(piece_rows, head_weight, preferred_element_type=jnp.float32)
    row_peak = jnp.max(logits, axis=1)
    shifted = logits - row_peak[:, None]
    exponent = jnp.exp(shifted)
    row_total = jnp.sum(exponent, axis=1)
    spread = jnp.sum(exponent * shifted, axis=1)
    column = lax.broadcasted_iota(jnp.int32, logits.shape, 1) + vocab_start
    picked = jnp.sum(jnp.where(column == piece_targets[:, None], logits, 0.0), axis=1)
    return (row_peak, row_total, spread, picked)


def blocked_stats(piece_rows, piece_targets, head_weight, vocab_start):
    row_count = piece_rows.shape[0]

    def one_block(block_pair):
        return piece_stats(block_pair[0], block_pair[1], head_weight, vocab_start)

    stacked = lax.map(
        one_block,
        (
            piece_rows.reshape(row_count // block_rows, block_rows, piece_rows.shape[1]),
            piece_targets.reshape(row_count // block_rows, block_rows),
        ),
    )
    return tuple((stat_block.reshape(row_count) for stat_block in stacked))


def rescale(group_stats, peak_all):
    row_peak, row_total, spread, picked = group_stats
    factor = jnp.exp(row_peak - peak_all)
    return (row_total * factor, factor * (spread + (row_peak - peak_all) * row_total), picked)


def local(hidden_states, norm_gain, head_weight, targets, lengths, slot_of):
    seq_count = lengths.shape[0]
    seq_len = hidden_states.shape[0] // seq_count
    vocab_index = lax.axis_index("vocab")
    vocab_start = vocab_index * head_weight.shape[1]
    position = lax.broadcasted_iota(jnp.int32, (seq_count, seq_len), 1)
    live_mask = position < lengths[:, None]
    held_rows = seq_count * seq_len
    sent_rows = normalize(hidden_states, norm_gain)
    fresh = blocked_stats(
        lax.all_gather(sent_rows, "vocab", axis=0, tiled=True),
        lax.all_gather(targets, "vocab", axis=0, tiled=True),
        head_weight,
        vocab_start,
    )
    group_stats = tuple((new_part for new_part in fresh))
    owner_start = vocab_index * held_rows
    peak_all = lax.pmax(group_stats[0], "vocab")
    scaled_total, scaled_spread, picked_all = rescale(group_stats, peak_all)
    summed = lax.psum((scaled_total, scaled_spread, picked_all), "vocab")
    row_total, spread, picked = tuple(
        (lax.dynamic_slice_in_dim(summed_part, owner_start, held_rows) for summed_part in summed)
    )
    global_peak = lax.dynamic_slice_in_dim(peak_all, owner_start, held_rows)
    log_total = jnp.log(row_total)
    own_logprob = picked - global_peak - log_total
    own_entropy = log_total - spread / row_total
    slot_logprob = own_logprob.reshape(seq_count, seq_len)
    slot_entropy = own_entropy.reshape(seq_count, seq_len)
    slot_logprob = jnp.where(live_mask, slot_logprob, 0.0)
    slot_entropy = jnp.where(live_mask, slot_entropy, 0.0)
    all_logprob, all_entropy = (
        lax.all_gather(slot_logprob, ("req", "vocab"), axis=0, tiled=True),
        lax.all_gather(slot_entropy, ("req", "vocab"), axis=0, tiled=True),
    )
    return (all_logprob[slot_of], all_entropy[slot_of])


def solution(mesh):
    in_specs = (
        P(("req", "vocab"), None),
        P(),
        P(None, "vocab"),
        P(("req", "vocab")),
        P(("req", "vocab")),
        P(("req", "vocab")),
    )
    out_specs = (P(("req", "vocab"), None), P(("req", "vocab"), None))
    return jax.shard_map(local, mesh=mesh, in_specs=in_specs, out_specs=out_specs, check_vma=False)
```

profile of v0, /device:TPU:0, one launch (start us, length us, event | category | flops | bytes accessed | tf_op | source)
XLA Modules:
  0.0 229.4 jit_solution(13073210896427432532)
XLA Ops:
  7.2 1.4 fusion.5
  8.6 2.3 fusion.7
  10.9 1.2 dynamic-slice
  12.8 0.9 dynamic-update-slice
  13.7 9.6 %all-reduce = s32[1536]{0:T(1024)S(1)} all-reduce(s32[1536]{0:T(1024)S(1)} %dynamic-update-slice), channel_id=1, replica_groups=mesh['req'=4,'vocab'=8] {'vocab'}, use_global_device_ids=true, to_apply=%add | all-reduce | flops 1536 | bytes 12288
  23.3 0.7 compare_select_fusion
  24.0 35.3 %all-gather.2.cloned.1.call-done = bf16[1536,2048]{1,0:T(8,128)(2,1)} async-done(((bf16[192,2048]{1,0:T(8,128)(2,1)}), bf16[1536,2048]{1,0:T(8,128)(2,1)}) %all-gather.2.cloned.1.call-update) | async-done | bytes 6291472 | tf_op jit(solution)/shard_map/all_gather | solution.py:60
  59.3 48.7 %while.16 = (s32[]{:T(128)}, f32[3,512]{1,0:T(4,128)S(1)}, f32[3,512]{1,0:T(4,128)S(1)}, f32[3,512]{1,0:T(4,128)S(1)}, f32[3,512]{1,0:T(4,128)S(1)}, /*index=5*/...) while((s32[]{:T(128)}, f32[3,512]{1,0:T(4,128)S(1)}, ...), condition=%wide.region_6.7_spmd, body=%wide.region_1.6_spmd.sunk | while | flops 8404994048 | bytes 34930564 | solution.py:34
  59.3 12.7 %fusion.16 = (f32[512]{0:T(512)S(1)}, f32[512,4000]{0,1:T(8,128)S(1)}) fusion(bf16[2048,4000]{0,1:T(8,128)(2,1)} %get-tuple-element.181, bf16[3,512,2048]{2,1,0:T(8,128)(2,1)} %get-tuple-element.180, s32[]{:T(128)} %get-tuple-element.164), kind=kOutput, calls=%fused_computation.27.clone.1 | convolution fusion | flops 8390655488 | bytes 26675712 | tf_op jit(solution)/shard_map/while/body/eval_jaxpr/dot_general | solution.py:17
  72.0 3.3 %fusion.17 = (f32[512]{0:T(512)S(1)}, f32[512]{0:T(512)S(1)}, f32[512]{0:T(512)S(1)}) fusion(f32[512,4000]{0,1:T(8,128)S(1)} %get-tuple-element.149, f32[512]{0:T(512)S(1)} %get-tuple-element.148, s32[512]{0:T(512)S(1)} %bitcast.31, s32[4000]{0:T(1024)S(1)} %iota_add_fusion.2), kind=kLoop, calls=%fused_computation.4.clone.1 | loop fusion | flops 14334464 | bytes 8218240 | tf_op jit(solution)/shard_map/while/body/eval_jaxpr/reduce_sum | solution.py:22
  75.3 0.1 dynamic_update_slice.19
  75.3 0.1 dynamic_update_slice.20
  75.4 0.1 dynamic_update_slice.18
  75.4 0.1 dynamic_update_slice.17
  75.5 12.7 %fusion.16 = (f32[512]{0:T(512)S(1)}, f32[512,4000]{0,1:T(8,128)S(1)}) fusion(bf16[2048,4000]{0,1:T(8,128)(2,1)} %get-tuple-element.181, bf16[3,512,2048]{2,1,0:T(8,128)(2,1)} %get-tuple-element.180, s32[]{:T(128)} %get-tuple-element.164), kind=kOutput, calls=%fused_computation.27.clone.1 | convolution fusion | flops 8390655488 | bytes 26675712 | tf_op jit(solution)/shard_map/while/body/eval_jaxpr/dot_general | solution.py:17
  88.3 3.3 %fusion.17 = (f32[512]{0:T(512)S(1)}, f32[512]{0:T(512)S(1)}, f32[512]{0:T(512)S(1)}) fusion(f32[512,4000]{0,1:T(8,128)S(1)} %get-tuple-element.149, f32[512]{0:T(512)S(1)} %get-tuple-element.148, s32[512]{0:T(512)S(1)} %bitcast.31, s32[4000]{0:T(1024)S(1)} %iota_add_fusion.2), kind=kLoop, calls=%fused_computation.4.clone.1 | loop fusion | flops 14334464 | bytes 8218240 | tf_op jit(solution)/shard_map/while/body/eval_jaxpr/reduce_sum | solution.py:22
  91.5 0.1 dynamic_update_slice.19
  91.6 0.1 dynamic_update_slice.20
  91.6 0.1 dynamic_update_slice.18
  91.8 12.7 %fusion.16 = (f32[512]{0:T(512)S(1)}, f32[512,4000]{0,1:T(8,128)S(1)}) fusion(bf16[2048,4000]{0,1:T(8,128)(2,1)} %get-tuple-element.181, bf16[3,512,2048]{2,1,0:T(8,128)(2,1)} %get-tuple-element.180, s32[]{:T(128)} %get-tuple-element.164), kind=kOutput, calls=%fused_computation.27.clone.1 | convolution fusion | flops 8390655488 | bytes 26675712 | tf_op jit(solution)/shard_map/while/body/eval_jaxpr/dot_general | solution.py:17
  104.5 3.3 %fusion.17 = (f32[512]{0:T(512)S(1)}, f32[512]{0:T(512)S(1)}, f32[512]{0:T(512)S(1)}) fusion(f32[512,4000]{0,1:T(8,128)S(1)} %get-tuple-element.149, f32[512]{0:T(512)S(1)} %get-tuple-element.148, s32[512]{0:T(512)S(1)} %bitcast.31, s32[4000]{0:T(1024)S(1)} %iota_add_fusion.2), kind=kLoop, calls=%fused_computation.4.clone.1 | loop fusion | flops 14334464 | bytes 8218240 | tf_op jit(solution)/shard_map/while/body/eval_jaxpr/reduce_sum | solution.py:22
  107.9 0.1 dynamic_update_slice.18
  108.0 13.4 %pmax.7 = f32[1536]{0:T(1024)S(1)} all-reduce(f32[1536]{0:T(1024)S(1)} %reshape.44), channel_id=1, replica_groups=mesh['req'=4,'vocab'=8] {'vocab'}, use_global_device_ids=true, to_apply=%region_8.9 | all-reduce | flops 1536 | bytes 12288 | tf_op jit(solution)/shard_map/pmax | solution.py:67
  121.5 22.4 %all-reduce.1 = (f32[1536]{0:T(1024)S(1)}, f32[1536]{0:T(1024)S(1)}, f32[1536]{0:T(1024)S(1)}) all-reduce(f32[1536]{0:T(1024)S(1)} %reshape.43, f32[1536]{0:T(1024)S(1)} %get-tuple-element.83, f32[1536]{0:T(1024)S(1)} %get-tuple-element.82), channel_id=1, replica_groups=mesh['req'=4,'vocab'=8] {'vocab'}, use_global_device_ids=true, to_apply=%region_7.8 | all-reduce | flops 4608 | bytes 36864 | tf_op jit(solution)/shard_map/psum | solution.py:69
  143.9 0.1 divide_subtract_fusion
  143.9 0.1 reshape.46
  144.0 0.1 reshape.48
  144.1 0.1 fusion.8
  144.2 39.2 %all_gather.14 = f32[256,24]{1,0:T(8,128)S(1)} all-gather(f32[8,24]{1,0:T(8,128)S(1)} %get-tuple-element.87), channel_id=1, replica_groups=mesh['req'=4,'vocab'=8] {'req','vocab'}, dimensions={0}, use_global_device_ids=true | all-gather | bytes 25344 | tf_op jit(solution)/shard_map/all_gather | solution.py:82
  183.4 37.0 %all_gather.15 = f32[256,24]{1,0:T(8,128)S(1)} all-gather(f32[8,24]{1,0:T(8,128)S(1)} %get-tuple-element.86), channel_id=1, replica_groups=mesh['req'=4,'vocab'=8] {'req','vocab'}, dimensions={0}, use_global_device_ids=true | all-gather | bytes 25344 | tf_op jit(solution)/shard_map/all_gather | solution.py:83
  220.3 1.1 gather_fusion
  221.5 1.1 gather_fusion.1
  (27 shorter events, 0.4 us)
Async XLA Ops:
  7.2 52.1 %all-gather.2.cloned.1.call-start = ((), (), s32[]{:S(2)}) async-start(), calls=%async_computation | async-start | bytes 7077888 | tf_op jit(solution)/shard_map/all_gather | solution.py:60
  59.3 84.8 %copy-start = (s32[8]{0:T(128)S(1)}, s32[8]{0:T(128)}, u32[]{:S(2)}) copy-start(s32[8]{0:T(128)} %param.12) | copy-start | bytes 100
Sparse Core Ops, SparseCore 0:
  11.0 48.2 all-gather.1
where the time goes:
time: 230 us; the launch traced here: 229 us
  blocking collectives  121 us (53%)
  matrix products  38.1 us (17%)
  waiting for transfers between devices  35.3 us (15%)
  between operations  14.8 us (6%)
  other arithmetic  14.3 us (6%)
  local copies, waits for them, and re-layouts  5.26 us (2%)
    all_gather x1, blocking collectives, local(): lax.all_gather(slot_logprob, ('req', 'vocab'), axis=0, tiled=True)  39.2 us
    dot_general x3, matrix products, piece_stats(): jnp.dot(piece_rows, head_weight, preferred_element_type=jnp.float32)  38.1 us
    all_gather x1, blocking collectives, local(): lax.all_gather(slot_entropy, ('req', 'vocab'), axis=0, tiled=True)  37 us
    all_gather x1, waiting for transfers between devices, local(): lax.all_gather(sent_rows, 'vocab', axis=0, tiled=True)  35.3 us
    psum x1, blocking collectives, local(): summed = lax.psum((scaled_total, scaled_spread, picked_all), 'vocab')  22.4 us
    pmax x1, blocking collectives, local(): peak_all = lax.pmax(group_stats[0], 'vocab')  13.4 us
    reduce_sum x3, other arithmetic, piece_stats(): spread = jnp.sum(exponent * shifted, axis=1)  9.8 us
    unnamed x1, blocking collectives  9.58 us
  transfers between devices with their start and end apart: 1, of which 1 were waited for; matrix products, arithmetic and copies ran while one was open for 1% of the time, Pallas kernels for 0%

commit v1 on v0

v1 whole, which is shorter than its diff:
```python
import functools

import jax
import jax.numpy as jnp
from jax import lax
from jax.experimental import pallas as pl
from jax.experimental.pallas import tpu as pltpu
from jax.sharding import PartitionSpec as P

eps_norm = 1e-05
live_cap = 128
extra = 16
tile_vocab = 800
part_vocab = 400
piece_rows = 256
lowest = -1e30
vmem_bytes = 40 * 1024 * 1024
f32 = jnp.float32


def prepare_kernel(lengths_ref, hidden_ref, gain_ref, targets_ref, out_ref):
    rows, depth = hidden_ref.shape
    seq_count = lengths_ref.shape[0]
    seq_len = rows // seq_count
    values = hidden_ref[...].astype(f32)
    inverse_rms = lax.rsqrt(jnp.mean(values * values, axis=1, keepdims=True) + eps_norm)
    normed = (values * inverse_rms * gain_ref[...]).astype(jnp.bfloat16)
    row = lax.broadcasted_iota(jnp.int32, (1, rows), 1)
    sublane = lax.broadcasted_iota(jnp.int32, (extra, live_cap), 0)
    lane = lax.broadcasted_iota(jnp.int32, (extra, live_cap), 1)
    place = jnp.full((1, rows), -1, jnp.int32)
    meta = jnp.zeros((extra, live_cap), jnp.int32)
    start = jnp.int32(0)
    for request in range(seq_count):
        length = lengths_ref[request]
        first = request * seq_len
        place = jnp.where((row >= first) & (row < first + length), row - first + start, place)
        meta = jnp.where(lane == request, start, meta)
        meta = jnp.where(lane == seq_count + request, length, meta)
        start = start + length
    chosen = lax.broadcasted_iota(jnp.int32, (live_cap, rows), 0) == place
    selector = chosen.astype(f32).astype(jnp.bfloat16)
    kept = jnp.dot(selector, normed, preferred_element_type=f32)
    for first in range(0, depth, 128):
        out_ref[first : first + 128, :] = kept[:, first : first + 128].T.astype(jnp.bfloat16)
    target = jnp.sum(jnp.where(chosen, targets_ref[...], 0), axis=1, keepdims=True)
    target = jnp.broadcast_to(target.astype(f32), (live_cap, 128)).T[:extra].astype(jnp.int32)
    meta = jnp.where(sublane == 0, target >> 8, meta)
    meta = jnp.where(sublane == 1, target & 255, meta)
    out_ref[depth:, :] = meta.astype(f32).astype(jnp.bfloat16)


def prepare(hidden_states, norm_gain, targets, lengths):
    rows, depth = hidden_states.shape
    return pl.pallas_call(
        prepare_kernel,
        out_shape=jax.ShapeDtypeStruct((depth + extra, live_cap), jnp.bfloat16),
        in_specs=[
            pl.BlockSpec(memory_space=pltpu.SMEM),
            pl.BlockSpec(memory_space=pltpu.VMEM),
            pl.BlockSpec(memory_space=pltpu.VMEM),
            pl.BlockSpec(memory_space=pltpu.VMEM),
        ],
        out_specs=pl.BlockSpec(memory_space=pltpu.VMEM),
        compiler_params=pltpu.CompilerParams(vmem_limit_bytes=vmem_bytes),
        name="prepare_rows",
    )(lengths, hidden_states, norm_gain.reshape(1, depth), targets.reshape(1, rows))


def stats_kernel(block_count, vocab_cols, steps, *refs):
    blocks = refs[:block_count]
    weight_ref = refs[block_count]
    out_ref, meta_ref = refs[-10:-8]
    rows_ref, logits_ref, peak_ref, total_ref, spread_ref, picked_ref, offset_ref, sems = refs[-8:]
    depth = weight_ref.shape[1]
    rows = block_count * live_cap
    halves = tile_vocab // part_vocab
    units = rows // piece_rows * halves
    step = pl.program_id(0)
    vocab_start = lax.axis_index("vocab") * vocab_cols
    last_valid = vocab_cols - (steps - 1) * tile_vocab

    @pl.when(step == 0)
    def _():
        copies = [
            pltpu.make_async_copy(block, rows_ref.at[:, pl.ds(place * live_cap, live_cap)], sems.at[place])
            for place, block in enumerate(blocks)
        ]
        for copy in copies:
            copy.start()
        peak_ref[...] = jnp.full(peak_ref.shape, lowest, f32)
        total_ref[...] = jnp.zeros(total_ref.shape, f32)
        spread_ref[...] = jnp.zeros(spread_ref.shape, f32)
        picked_ref[...] = jnp.zeros(picked_ref.shape, f32)
        logits_ref[(units - 1) % 2] = jnp.full(logits_ref.shape[1:], lowest, f32)
        for copy in copies:
            copy.wait()
        digits = rows_ref[depth:, :].astype(f32)
        target = (digits[0:1] * 256.0 + digits[1:2]).astype(jnp.int32) - vocab_start
        target = jnp.where((target >= 0) & (target < vocab_cols), target, 2 * steps * tile_vocab)
        offset_ref[...] = target - lax.broadcasted_iota(jnp.int32, (8, rows), 0)
        meta_ref[...] = digits[2:3]

    def absorb(unit, tile):
        slot = unit % 2
        piece, half = divmod(unit, halves)
        base = half * part_vocab
        sublane = lax.broadcasted_iota(jnp.int32, (8, 128), 0)
        for part in range(piece_rows // 128):
            own = pl.ds(piece * piece_rows + part * 128, 128)

            def load(group):
                values = logits_ref[slot, pl.ds(group * 8, 8), pl.ds(part * 128, 128)]
                if base + (group + 1) * 8 > last_valid:
                    left = vocab_cols - tile * tile_vocab - base - group * 8
                    values = jnp.where(sublane < left, values, lowest)
                return values

            groups = part_vocab // 8
            ways = 4
            tops = [load(group) for group in range(ways)]
            for group in range(ways, groups):
                tops[group % ways] = jnp.maximum(tops[group % ways], load(group))
            before = peak_ref[:, own]
            peak = functools.reduce(jnp.maximum, tops, before)
            change = before - peak
            factor = jnp.exp(change)
            total = total_ref[:, own]
            spread = factor * (spread_ref[:, own] + change * total)
            total = total * factor
            picked = picked_ref[:, own]
            offset = offset_ref[:, own]
            totals = [total] + [jnp.zeros_like(total)] * (ways - 1)
            spreads = [spread] + [jnp.zeros_like(total)] * (ways - 1)
            for group in range(groups):
                values = load(group)
                shifted = values - peak
                exponent = jnp.exp(shifted)
                totals[group % ways] = totals[group % ways] + exponent
                spreads[group % ways] = spreads[group % ways] + exponent * shifted
                picked = jnp.where(offset == tile * tile_vocab + base + group * 8, values, picked)
            peak_ref[:, own] = peak
            total_ref[:, own] = (totals[0] + totals[1]) + (totals[2] + totals[3])
            spread_ref[:, own] = (spreads[0] + spreads[1]) + (spreads[2] + spreads[3])
            picked_ref[:, own] = picked

    for unit in range(units):
        piece, half = divmod(unit, halves)
        logits_ref[unit % 2] = jnp.dot(
            weight_ref[pl.ds(half * part_vocab, part_vocab), :],
            rows_ref[:depth, pl.ds(piece * piece_rows, piece_rows)],
            preferred_element_type=f32,
        )
        if unit == 0:
            absorb(units - 1, step - 1)
        else:
            absorb(unit - 1, step)

    @pl.when(step == steps - 1)
    def _():
        absorb(units - 1, step)
        peak = peak_ref[...]
        total = total_ref[...]
        top = jnp.max(peak, axis=0, keepdims=True)
        change = peak - top
        factor = jnp.exp(change)
        out_ref[0:1, :] = top
        out_ref[1:2, :] = jnp.sum(total * factor, axis=0, keepdims=True)
        out_ref[2:3, :] = jnp.sum(factor * (spread_ref[...] + change * total), axis=0, keepdims=True)
        out_ref[3:4, :] = jnp.sum(picked_ref[...], axis=0, keepdims=True)


def block_stats(blocks, weight_rows):
    count = len(blocks)
    rows = count * live_cap
    vocab_cols, depth = weight_rows.shape
    steps = -(-vocab_cols // tile_vocab)
    return pl.pallas_call(
        functools.partial(stats_kernel, count, vocab_cols, steps),
        grid=(steps,),
        out_shape=(jax.ShapeDtypeStruct((4, rows), f32), jax.ShapeDtypeStruct((1, rows), f32)),
        in_specs=[pl.BlockSpec(memory_space=pl.ANY)] * count
        + [pl.BlockSpec((tile_vocab, depth), lambda step: (step, 0))],
        out_specs=(
            pl.BlockSpec((4, rows), lambda step: (0, 0)),
            pl.BlockSpec((1, rows), lambda step: (0, 0)),
        ),
        scratch_shapes=[
            pltpu.VMEM((depth + extra, rows), jnp.bfloat16),
            pltpu.VMEM((2, part_vocab, piece_rows), f32),
            pltpu.VMEM((8, rows), f32),
            pltpu.VMEM((8, rows), f32),
            pltpu.VMEM((8, rows), f32),
            pltpu.VMEM((8, rows), f32),
            pltpu.VMEM((8, rows), jnp.int32),
            pltpu.SemaphoreType.DMA((count,)),
        ],
        compiler_params=pltpu.CompilerParams(
            vmem_limit_bytes=vmem_bytes, dimension_semantics=("arbitrary",)
        ),
        cost_estimate=pl.CostEstimate(
            flops=2 * rows * depth * vocab_cols,
            bytes_accessed=2 * depth * vocab_cols,
            transcendentals=rows * vocab_cols,
        ),
        name="row_stats",
    )(*blocks, weight_rows)


def combine_kernel(order, *refs):
    peers = refs[: len(order)]
    meta_ref, out_ref = refs[len(order) :]
    for place in range(len(order[0])):
        own = pl.ds(place * live_cap, live_cap)
        parts = [peer[:, pl.ds(order[j][place] * live_cap, live_cap)] for j, peer in enumerate(peers)]
        top = functools.reduce(jnp.maximum, [part[0:1] for part in parts])
        total = jnp.zeros_like(top)
        spread = jnp.zeros_like(top)
        picked = jnp.zeros_like(top)
        for part in parts:
            change = part[0:1] - top
            factor = jnp.exp(change)
            total = total + part[1:2] * factor
            spread = spread + factor * (part[2:3] + change * part[1:2])
            picked = picked + part[3:4]
        log_total = jnp.log(total)
        out_ref[0:1, own] = picked - top - log_total
        out_ref[1:2, own] = log_total - spread / total
        out_ref[2:3, own] = meta_ref[:, own]
        out_ref[3:8, own] = jnp.zeros((5, live_cap), f32)


def combine(peers, order, meta):
    rows = meta.shape[1]
    return pl.pallas_call(
        functools.partial(combine_kernel, order),
        out_shape=jax.ShapeDtypeStruct((8, rows), f32),
        in_specs=[pl.BlockSpec(memory_space=pltpu.VMEM)] * (len(peers) + 1),
        out_specs=pl.BlockSpec(memory_space=pltpu.VMEM),
        compiler_params=pltpu.CompilerParams(vmem_limit_bytes=vmem_bytes),
        name="combine_stats",
    )(*peers, meta)


def pick_kernel(vocab_count, req_count, paired, seq_len, slot_ref, *refs):
    groups = refs[:req_count]
    logprob_ref, entropy_ref = refs[req_count:]
    seq_count = slot_ref.shape[0]
    req = lax.axis_index("req")
    vocab = lax.axis_index("vocab")
    lane = lax.broadcasted_iota(jnp.int32, (8, 128), 1)
    sublane = lax.broadcasted_iota(jnp.int32, (8, 128), 0)
    for request in range(seq_count):
        slot = slot_ref[request]
        owner = slot // seq_count
        within = slot - owner * seq_count
        owner_req = owner // vocab_count
        place = owner - owner_req * vocab_count
        if paired:
            place = place ^ vocab
        behind = lax.rem(req - owner_req + req_count, req_count)
        columns = pl.ds(pl.multiple_of(place * live_cap, live_cap), live_cap)
        block = groups[0][:, columns]
        for j in range(1, req_count):
            block = jnp.where(behind == j, groups[j][:, columns], block)
        meta = jnp.where(sublane == 2, block, 0.0)
        start = jnp.sum(jnp.where(lane == within, meta, 0.0), keepdims=True).astype(jnp.int32)
        length = jnp.sum(jnp.where(lane == seq_count + within, meta, 0.0), keepdims=True).astype(jnp.int32)
        index = jnp.minimum(start + lane, live_cap - 1)
        found = jnp.take_along_axis(block, index, axis=1, mode="promise_in_bounds")
        found = jnp.where(lane < length, found, 0.0)
        logprob_ref[request : request + 1, :] = found[0:1, :seq_len]
        entropy_ref[request : request + 1, :] = found[1:2, :seq_len]


def pick(slot_of, groups, vocab_count, paired, seq_len):
    shape = jax.ShapeDtypeStruct((slot_of.shape[0], seq_len), f32)
    return pl.pallas_call(
        functools.partial(pick_kernel, vocab_count, len(groups), paired, seq_len),
        out_shape=(shape, shape),
        in_specs=[pl.BlockSpec(memory_space=pltpu.SMEM)]
        + [pl.BlockSpec(memory_space=pltpu.VMEM)] * len(groups),
        out_specs=(pl.BlockSpec(memory_space=pltpu.VMEM), pl.BlockSpec(memory_space=pltpu.VMEM)),
        compiler_params=pltpu.CompilerParams(vmem_limit_bytes=vmem_bytes),
        name="pick_requests",
    )(slot_of, *groups)


def swap(array, mask, count):
    return lax.ppermute(array, "vocab", [(i, i ^ mask) for i in range(count)])


def local(vocab_count, req_count, hidden_states, norm_gain, head_weight, targets, lengths, slot_of):
    seq_len = hidden_states.shape[0] // lengths.shape[0]
    own = prepare(hidden_states, norm_gain, targets, lengths)
    weight_rows = head_weight.T
    paired = vocab_count == 8
    if paired:
        x_same = swap(own, 2, vocab_count)
        y_same = swap(own, 4, vocab_count)
        core = swap(own, 1, vocab_count)
        first = block_stats((own, core), weight_rows)
        x_other = swap(x_same, 1, vocab_count)
        y_other = swap(y_same, 1, vocab_count)
        half = own.shape[0] // 32 * 16
        diagonal = jnp.concatenate(
            (swap(x_same[:half], 4, vocab_count), swap(y_same[half:], 2, vocab_count)), axis=0
        )
        second = block_stats((x_same, x_other, y_same, y_other), weight_rows)
        diagonal_other = swap(diagonal, 1, vocab_count)
        third = block_stats((diagonal, diagonal_other), weight_rows)
        calls = (first, second, third)
        order = [[k ^ j for k in range(vocab_count)] for j in range(vocab_count)]
    else:
        gathered = lax.all_gather(own, "vocab", axis=0)
        calls = [
            block_stats([gathered[k] for k in range(at, min(at + 4, vocab_count))], weight_rows)
            for at in range(0, vocab_count, 4)
        ]
        order = [list(range(vocab_count))] * vocab_count
    stats = jnp.concatenate([call[0] for call in calls], axis=1)
    meta = jnp.concatenate([call[1] for call in calls], axis=1)
    if paired:
        peers = [stats] + [swap(stats, j, vocab_count) for j in range(1, vocab_count)]
    else:
        everyone = lax.all_gather(stats, "vocab", axis=0)
        peers = [everyone[j] for j in range(vocab_count)]
    result = combine(peers, order, meta)
    groups = [result] + [
        lax.ppermute(result, "req", [(i, (i + j) % req_count) for i in range(req_count)])
        for j in range(1, req_count)
    ]
    return pick(slot_of, groups, vocab_count, paired, seq_len)


def solution(mesh):
    in_specs = (
        P(("req", "vocab"), None),
        P(),
        P(None, "vocab"),
        P(("req", "vocab")),
        P(("req", "vocab")),
        P(("req", "vocab")),
    )
    out_specs = (P(("req", "vocab"), None), P(("req", "vocab"), None))
    body = functools.partial(local, mesh.shape["vocab"], mesh.shape["req"])
    return jax.shard_map(body, mesh=mesh, in_specs=in_specs, out_specs=out_specs, check_vma=False)
```

time: 230 us -> 76.1 us (0.33)
  blocking collectives: 121 us -> 0 us
  matrix products: 38.1 us -> 0 us
  Pallas kernels: 0 us -> 35.2 us
  starting transfers between devices: 0.04 us -> 20.4 us
  waiting for transfers between devices: 35.3 us -> 16 us
  other arithmetic: 14.3 us -> 0.01 us
  between operations: 14.8 us -> 0.79 us
    all_gather x2 -> x0, blocking collectives: 76.1 us -> none  [the longest x1 39.2 us: local(): lax.all_gather(slot_logprob, ('req', 'vocab'), axis=0, tiled=True)]
    dot_general x3 -> x0, matrix products: 38.1 us -> none  [piece_stats(): jnp.dot(piece_rows, head_weight, preferred_element_type=jnp.float32)]
    all_gather x1 -> x0, waiting for transfers between devices: 35.3 us -> none  [local(): lax.all_gather(sent_rows, 'vocab', axis=0, tiled=True)]
    pallas_call x0 -> x6, Pallas kernels: none -> 35.2 us  [the longest x3 32.3 us: block_stats(): pl.pallas_call(functools.partial(stats_kernel, count, vocab_cols, steps),...]
    psum x1 -> x0, blocking collectives: 22.4 us -> none  [local(): summed = lax.psum((scaled_total, scaled_spread, picked_all), 'vocab')]
    ppermute x0 -> x18, starting transfers between devices: none -> 20.4 us  [the longest x15 14.8 us: swap(): return lax.ppermute(array, 'vocab', [(i, i ^ mask) for i in range(count)])]
    ppermute x0 -> x18, waiting for transfers between devices: none -> 16 us  [the longest x15 13.5 us: swap(): return lax.ppermute(array, 'vocab', [(i, i ^ mask) for i in range(count)])]
    pmax x1 -> x0, blocking collectives: 13.4 us -> none  [local(): peak_all = lax.pmax(group_stats[0], 'vocab')]
  transfers between devices with their start and end apart: 1 -> 18, of which waited for: 1 -> 6; matrix products, arithmetic and copies ran while one was open for 1% -> 0% of each run, Pallas kernels for 0% -> 30%
where the time goes in v1:
time: 76.1 us; the launch traced here: 75.7 us
  Pallas kernels  35.2 us (46%)
  starting transfers between devices  20.4 us (27%)
  waiting for transfers between devices  16 us (21%)
  local copies, waits for them, and re-layouts  3.27 us (4%)
  between operations  0.79 us (1%)
    pallas_call x3, Pallas kernels, block_stats(): pl.pallas_call(functools.partial(stats_kernel, count, vocab_cols, steps),...  32.3 us
    ppermute x15, starting transfers between devices, swap(): return lax.ppermute(array, 'vocab', [(i, i ^ mask) for i in range(count)])  14.8 us
    ppermute x15, waiting for transfers between devices, swap(): return lax.ppermute(array, 'vocab', [(i, i ^ mask) for i in range(count)])  13.5 us
    ppermute x3, starting transfers between devices, local(): lax.ppermute(result, 'req', [(i, (i + j) % req_count) for i in range(req_...  5.56 us
    unnamed x13, local copies, waits for them, and re-layouts  3.19 us
    ppermute x3, waiting for transfers between devices, local(): lax.ppermute(result, 'req', [(i, (i + j) % req_count) for i in range(req_...  2.57 us
  transfers between devices with their start and end apart: 18, of which 6 were waited for; matrix products, arithmetic and copies ran while one was open for 0% of the time, Pallas kernels for 30%

profile of v1, /device:TPU:0, one launch (start us, length us, event | category | flops | bytes accessed | tf_op | source)
XLA Modules:
  0.0 75.7 jit_solution(1371099161984199931)
XLA Ops:
  0.6 1.1 %copy-done = bf16[192,2048]{1,0:T(8,128)(2,1)S(1)} copy-done((bf16[192,2048]{1,0:T(8,128)(2,1)S(1)}, bf16[192,2048]{1,0:T(8,128)(2,1)}, u32[]{:S(2)}) %copy-start) | copy-done | bytes 786456
  1.8 0.7 copy-done.1
  2.5 0.7 copy-done.2
  3.1 0.7 copy-done.3
  3.8 1.2 %prepare_rows.1.refs_0_ = bf16[2064,128]{1,0:T(8,128)(2,1)S(1)} custom-call(s32[8]{0:T(128)S(1)} %copy-done.3, bf16[192,2048]{1,0:T(8,128)(2,1)S(1)} %copy-done, f32[1,2048]{1,0:T(1,128)S(1)} %bitcast.3, s32[1,192]{1,0:T(1,128)S(1)} %bitcast.4), custom_call_target="tpu_custom_call" | custom-call | tf_op jit(solution)/shard_map/prepare_rows/pallas_call | solution.py:55
  5.0 3.0 %collective-permute-start.1 = (bf16[2064,128]{1,0:T(8,128)(2,1)S(1)}, bf16[2064,128]{1,0:T(8,128)(2,1)S(1)}, u32[]{:S(2)}, u32[]{:S(2)}) collective-permute-start(bf16[2064,128]{1,0:T(8,128)(2,1)S(1)} %prepare_rows.1.refs_0_), channel_id=1, source_target_pairs={{0,2},{1,3},{2,0},{3,1},{4,6},{5,7},{6,4},{7,5},{8,10},{9,11},{10,... | collective-permute-start | bytes 1585160 | tf_op jit(solution)/shard_map/ppermute | solution.py:290
  8.0 1.5 %collective-permute-start.3 = (bf16[2064,128]{1,0:T(8,128)(2,1)S(1)}, bf16[2064,128]{1,0:T(8,128)(2,1)S(1)}, u32[]{:S(2)}, u32[]{:S(2)}) collective-permute-start(bf16[2064,128]{1,0:T(8,128)(2,1)S(1)} %prepare_rows.1.refs_0_), channel_id=1, source_target_pairs={{0,4},{1,5},{2,6},{3,7},{4,0},{5,1},{6,2},{7,3},{8,12},{9,13},{10,... | collective-permute-start | bytes 1585160 | tf_op jit(solution)/shard_map/ppermute | solution.py:290
  9.5 10.5 %collective-permute-done.1.refs_0_ = bf16[2064,128]{1,0:T(8,128)(2,1)S(1)} collective-permute-done((bf16[2064,128]{1,0:T(8,128)(2,1)S(1)}, bf16[2064,128]{1,0:T(8,128)(2,1)S(1)}, u32[]{:S(2)}, u32[]{:S(2)}) %collective-permute-start.1) | collective-permute-done | bytes 528416 | tf_op jit(solution)/shard_map/ppermute | solution.py:290
  20.0 1.8 %collective-permute-start.5 = (bf16[1024,128]{1,0:T(8,128)(2,1)S(1)}, bf16[1024,128]{1,0:T(8,128)(2,1)S(1)}, u32[]{:S(2)}, u32[]{:S(2)}) collective-permute-start(bf16[1024,128]{1,0:T(8,128)(2,1)S(1)} %slice.8), channel_id=1, source_target_pairs={{0,4},{1,5},{2,6},{3,7},{4,0},{5,1},{6,2},{7,3},{8,12},{9,13},{10,... | collective-permute-start | bytes 786440 | tf_op jit(solution)/shard_map/ppermute | solution.py:290
  21.9 1.6 %collective-permute-start.6 = (bf16[1040,128]{1,0:T(8,128)(2,1)S(1)}, bf16[1040,128]{1,0:T(8,128)(2,1)S(1)}, u32[]{:S(2)}, u32[]{:S(2)}) collective-permute-start(bf16[1040,128]{1,0:T(8,128)(2,1)S(1)} %slice.9), channel_id=1, source_target_pairs={{0,2},{1,3},{2,0},{3,1},{4,6},{5,7},{6,4},{7,5},{8,10},{9,11},{10,... | collective-permute-start | bytes 798728 | tf_op jit(solution)/shard_map/ppermute | solution.py:290
  23.4 0.5 collective-permute-start.4
  23.9 9.7 %row_stats.3 = (f32[4,256]{1,0:T(4,128)S(1)}, f32[1,256]{1,0:T(1,128)S(1)}) custom-call(bf16[2064,128]{1,0:T(8,128)(2,1)S(1)} %prepare_rows.1.refs_0_, bf16[2064,128]{1,0:T(8,128)(2,1)S(1)} %collective-permute-done.refs_1_, bf16[4000,2048]{1,0:T(8,128)(2,1)} %bitcast.5), custom_call_target="tpu_custom_call" | custom-call | flops 4194304000 | bytes 16384000 | tf_op jit(solution)/shard_map/row_stats/pallas_call | solution.py:178
  33.8 0.1 collective-permute-start.7
  33.9 12.9 %row_stats.4 = (f32[4,512]{1,0:T(4,128)S(1)}, f32[1,512]{1,0:T(1,128)S(1)}) custom-call(bf16[2064,128]{1,0:T(8,128)(2,1)S(1)} %collective-permute-done.1.refs_0_, bf16[2064,128]{1,0:T(8,128)(2,1)S(1)} %collective-permute-done.2.refs_1_, bf16[2064,128]{1,0:T(8,128)(2,1)S(1)} %collective-permute-done.3.refs_2_, ...), custom_call_target="tpu_custom_call" | custom-call | flops 8388608000 | bytes 16384000 | tf_op jit(solution)/shard_map/row_stats/pallas_call | solution.py:178
  46.8 9.7 %row_stats.5 = (f32[4,256]{1,0:T(4,128)S(1)}, f32[1,256]{1,0:T(1,128)S(1)}) custom-call(bf16[2064,128]{1,0:T(8,128)(2,1)S(1)} %constant_dynamic-update-slice_fusion.refs_0_, bf16[2064,128]{1,0:T(8,128)(2,1)S(1)} %collective-permute-done.7.refs_1_, bf16[4000,2048]{1,0:T(8,128)(2,1)} %bitcast.7), custom_call_target="tpu_custom_call" | custom-call | flops 4194304000 | bytes 16384000 | tf_op jit(solution)/shard_map/row_stats/pallas_call | solution.py:178
  56.5 0.5 collective-permute-start.8
  57.1 0.5 collective-permute-start.9
  57.6 0.9 %collective-permute-start.10 = (f32[4,1024]{1,0:T(4,128)S(1)}, f32[4,1024]{1,0:T(4,128)S(1)}, u32[]{:S(2)}, u32[]{:S(2)}) collective-permute-start(f32[4,1024]{1,0:T(4,128)S(1)} %constant_dynamic-update-slice_fusion.2.refs_0_), channel_id=1, source_target_pairs={{0,3},{1,2},{2,1},{3,0},{4,7},{5,6},{6,5},{7,4},{8,11},{9,10},{10,... | collective-permute-start | bytes 49160 | tf_op jit(solution)/shard_map/ppermute | solution.py:290
  58.5 0.5 collective-permute-start.11
  59.0 1.6 %collective-permute-start.12 = (f32[4,1024]{1,0:T(4,128)S(1)}, f32[4,1024]{1,0:T(4,128)S(1)}, u32[]{:S(2)}, u32[]{:S(2)}) collective-permute-start(f32[4,1024]{1,0:T(4,128)S(1)} %constant_dynamic-update-slice_fusion.2.refs_0_), channel_id=1, source_target_pairs={{0,5},{1,4},{2,7},{3,6},{4,1},{5,0},{6,3},{7,2},{8,13},{9,12},{10,... | collective-permute-start | bytes 49160 | tf_op jit(solution)/shard_map/ppermute | solution.py:290
  60.6 1.1 %collective-permute-start.13 = (f32[4,1024]{1,0:T(4,128)S(1)}, f32[4,1024]{1,0:T(4,128)S(1)}, u32[]{:S(2)}, u32[]{:S(2)}) collective-permute-start(f32[4,1024]{1,0:T(4,128)S(1)} %constant_dynamic-update-slice_fusion.2.refs_0_), channel_id=1, source_target_pairs={{0,6},{1,7},{2,4},{3,5},{4,2},{5,3},{6,0},{7,1},{8,14},{9,15},{10,... | collective-permute-start | bytes 49160 | tf_op jit(solution)/shard_map/ppermute | solution.py:290
  61.7 1.2 %collective-permute-start.14 = (f32[4,1024]{1,0:T(4,128)S(1)}, f32[4,1024]{1,0:T(4,128)S(1)}, u32[]{:S(2)}, u32[]{:S(2)}) collective-permute-start(f32[4,1024]{1,0:T(4,128)S(1)} %constant_dynamic-update-slice_fusion.2.refs_0_), channel_id=1, source_target_pairs={{0,7},{1,6},{2,5},{3,4},{4,3},{5,2},{6,1},{7,0},{8,15},{9,14},{10,... | collective-permute-start | bytes 49160 | tf_op jit(solution)/shard_map/ppermute | solution.py:290
  62.9 2.3 %collective-permute-done.13.refs_6_ = f32[4,1024]{1,0:T(4,128)S(1)} collective-permute-done((f32[4,1024]{1,0:T(4,128)S(1)}, f32[4,1024]{1,0:T(4,128)S(1)}, u32[]{:S(2)}, u32[]{:S(2)}) %collective-permute-start.13) | collective-permute-done | bytes 16416 | tf_op jit(solution)/shard_map/ppermute | solution.py:290
  65.2 0.7 collective-permute-done.14.refs_7_
  65.9 0.2 combine_stats.1.refs_0_
  66.0 1.6 %collective-permute-start.15 = (f32[8,1024]{1,0:T(8,128)S(1)}, f32[8,1024]{1,0:T(8,128)S(1)}, u32[]{:S(2)}, u32[]{:S(2)}) collective-permute-start(f32[8,1024]{1,0:T(8,128)S(1)} %combine_stats.1.refs_0_), channel_id=1, source_target_pairs={{0,8},{8,16},{16,24},{24,0},{1,9},{9,17},{17,25},{25,1},{2,10},{10... | collective-permute-start | bytes 98312 | tf_op jit(solution)/shard_map/ppermute | solution.py:330
  67.7 2.6 %collective-permute-start.16 = (f32[8,1024]{1,0:T(8,128)S(1)}, f32[8,1024]{1,0:T(8,128)S(1)}, u32[]{:S(2)}, u32[]{:S(2)}) collective-permute-start(f32[8,1024]{1,0:T(8,128)S(1)} %combine_stats.1.refs_0_), channel_id=1, source_target_pairs={{0,16},{8,24},{16,0},{24,8},{1,17},{9,25},{17,1},{25,9},{2,18},{10... | collective-permute-start | bytes 98312 | tf_op jit(solution)/shard_map/ppermute | solution.py:330
  70.3 1.3 %collective-permute-start.17 = (f32[8,1024]{1,0:T(8,128)S(1)}, f32[8,1024]{1,0:T(8,128)S(1)}, u32[]{:S(2)}, u32[]{:S(2)}) collective-permute-start(f32[8,1024]{1,0:T(8,128)S(1)} %combine_stats.1.refs_0_), channel_id=1, source_target_pairs={{0,24},{8,0},{16,8},{24,16},{1,25},{9,1},{17,9},{25,17},{2,26},{10... | collective-permute-start | bytes 98312 | tf_op jit(solution)/shard_map/ppermute | solution.py:330
  71.6 0.2 collective-permute-done.15.refs_1_
  71.8 1.2 %collective-permute-done.16.refs_2_ = f32[8,1024]{1,0:T(8,128)S(1)} collective-permute-done((f32[8,1024]{1,0:T(8,128)S(1)}, f32[8,1024]{1,0:T(8,128)S(1)}, u32[]{:S(2)}, u32[]{:S(2)}) %collective-permute-start.16) | collective-permute-done | bytes 32800 | tf_op jit(solution)/shard_map/ppermute | solution.py:330
  73.0 1.2 %collective-permute-done.17.refs_3_ = f32[8,1024]{1,0:T(8,128)S(1)} collective-permute-done((f32[8,1024]{1,0:T(8,128)S(1)}, f32[8,1024]{1,0:T(8,128)S(1)}, u32[]{:S(2)}, u32[]{:S(2)}) %collective-permute-start.17) | collective-permute-done | bytes 32800 | tf_op jit(solution)/shard_map/ppermute | solution.py:330
  74.2 1.5 %pick_requests.1 = (f32[8,24]{1,0:T(8,128)}, f32[8,24]{1,0:T(8,128)}) custom-call(s32[8]{0:T(128)S(1)} %copy-done.4, f32[8,1024]{1,0:T(8,128)S(1)} %combine_stats.1.refs_0_, f32[8,1024]{1,0:T(8,128)S(1)} %collective-permute-done.15.refs_1_, f32[8,1024]{1,0:T(8,128)S(1)} %collective-permute-done.16.refs_2_, f32[8,1024]{1,0:T(8,128)S(1)} %collective-permute-done.17.refs_3_), custom_call_target="tpu_custom_call" | custom-call | tf_op jit(solution)/shard_map/pick_requests/pallas_call | solution.py:278
  (28 shorter events, 0.2 us)
Async XLA Ops:
  0.6 1.1 %copy-start = (bf16[192,2048]{1,0:T(8,128)(2,1)S(1)}, bf16[192,2048]{1,0:T(8,128)(2,1)}, u32[]{:S(2)}) copy-start(bf16[192,2048]{1,0:T(8,128)(2,1)} %hidden_ref.1) | copy-start | bytes 2359300
  1.8 0.7 copy-start.1
  2.5 0.7 copy-start.2
  3.1 0.7 copy-start.3
  5.0 15.0 %collective-permute-start.1 = (bf16[2064,128]{1,0:T(8,128)(2,1)S(1)}, bf16[2064,128]{1,0:T(8,128)(2,1)S(1)}, u32[]{:S(2)}, u32[]{:S(2)}) collective-permute-start(bf16[2064,128]{1,0:T(8,128)(2,1)S(1)} %prepare_rows.1.refs_0_), channel_id=1, source_target_pairs={{0,2},{1,3},{2,0},{3,1},{4,6},{5,7},{6,4},{7,5},{8,10},{9,11},{10,... | collective-permute-start | bytes 1585160 | tf_op jit(solution)/shard_map/ppermute | solution.py:290
  8.0 13.9 %collective-permute-start.3 = (bf16[2064,128]{1,0:T(8,128)(2,1)S(1)}, bf16[2064,128]{1,0:T(8,128)(2,1)S(1)}, u32[]{:S(2)}, u32[]{:S(2)}) collective-permute-start(bf16[2064,128]{1,0:T(8,128)(2,1)S(1)} %prepare_rows.1.refs_0_), channel_id=1, source_target_pairs={{0,4},{1,5},{2,6},{3,7},{4,0},{5,1},{6,2},{7,3},{8,12},{9,13},{10,... | collective-permute-start | bytes 1585160 | tf_op jit(solution)/shard_map/ppermute | solution.py:290
  9.5 14.4 %collective-permute-start = (bf16[2064,128]{1,0:T(8,128)(2,1)S(1)}, bf16[2064,128]{1,0:T(8,128)(2,1)S(1)}, u32[]{:S(2)}, u32[]{:S(2)}) collective-permute-start(bf16[2064,128]{1,0:T(8,128)(2,1)S(1)} %prepare_rows.1.refs_0_), channel_id=1, source_target_pairs={{0,1},{1,0},{2,3},{3,2},{4,5},{5,4},{6,7},{7,6},{8,9},{9,8},{10,11... | collective-permute-start | bytes 1585160 | tf_op jit(solution)/shard_map/ppermute | solution.py:290
  20.0 13.7 %collective-permute-start.5 = (bf16[1024,128]{1,0:T(8,128)(2,1)S(1)}, bf16[1024,128]{1,0:T(8,128)(2,1)S(1)}, u32[]{:S(2)}, u32[]{:S(2)}) collective-permute-start(bf16[1024,128]{1,0:T(8,128)(2,1)S(1)} %slice.8), channel_id=1, source_target_pairs={{0,4},{1,5},{2,6},{3,7},{4,0},{5,1},{6,2},{7,3},{8,12},{9,13},{10,... | collective-permute-start | bytes 786440 | tf_op jit(solution)/shard_map/ppermute | solution.py:290
  21.9 11.9 %collective-permute-start.6 = (bf16[1040,128]{1,0:T(8,128)(2,1)S(1)}, bf16[1040,128]{1,0:T(8,128)(2,1)S(1)}, u32[]{:S(2)}, u32[]{:S(2)}) collective-permute-start(bf16[1040,128]{1,0:T(8,128)(2,1)S(1)} %slice.9), channel_id=1, source_target_pairs={{0,2},{1,3},{2,0},{3,1},{4,6},{5,7},{6,4},{7,5},{8,10},{9,11},{10,... | collective-permute-start | bytes 798728 | tf_op jit(solution)/shard_map/ppermute | solution.py:290
  23.4 10.4 %collective-permute-start.2 = (bf16[2064,128]{1,0:T(8,128)(2,1)S(1)}, bf16[2064,128]{1,0:T(8,128)(2,1)S(1)}, u32[]{:S(2)}, u32[]{:S(2)}) collective-permute-start(bf16[2064,128]{1,0:T(8,128)(2,1)S(1)} %collective-permute-done.1.refs_0_), channel_id=1, source_target_pairs={{0,1},{1,0},{2,3},{3,2},{4,5},{5,4},{6,7},{7,6},{8,9},{9,8},{10,11... | collective-permute-start | bytes 1585160 | tf_op jit(solution)/shard_map/ppermute | solution.py:290
  23.4 10.4 %collective-permute-start.4 = (bf16[2064,128]{1,0:T(8,128)(2,1)S(1)}, bf16[2064,128]{1,0:T(8,128)(2,1)S(1)}, u32[]{:S(2)}, u32[]{:S(2)}) collective-permute-start(bf16[2064,128]{1,0:T(8,128)(2,1)S(1)} %collective-permute-done.3.refs_2_), channel_id=1, source_target_pairs={{0,1},{1,0},{2,3},{3,2},{4,5},{5,4},{6,7},{7,6},{8,9},{9,8},{10,11... | collective-permute-start | bytes 1585160 | tf_op jit(solution)/shard_map/ppermute | solution.py:290
  33.8 13.0 %collective-permute-start.7 = (bf16[2064,128]{1,0:T(8,128)(2,1)S(1)}, bf16[2064,128]{1,0:T(8,128)(2,1)S(1)}, u32[]{:S(2)}, u32[]{:S(2)}) collective-permute-start(bf16[2064,128]{1,0:T(8,128)(2,1)S(1)} %constant_dynamic-update-slice_fusion.refs_0_), channel_id=1, source_target_pairs={{0,1},{1,0},{2,3},{3,2},{4,5},{5,4},{6,7},{7,6},{8,9},{9,8},{10,11... | collective-permute-start | bytes 1585160 | tf_op jit(solution)/shard_map/ppermute | solution.py:290
  46.8 27.4 %copy-start.4 = (s32[8]{0:T(128)S(1)}, s32[8]{0:T(128)}, u32[]{:S(2)}) copy-start(s32[8]{0:T(128)} %slot_ref.1) | copy-start | bytes 100
  56.5 4.1 %collective-permute-start.8 = (f32[4,1024]{1,0:T(4,128)S(1)}, f32[4,1024]{1,0:T(4,128)S(1)}, u32[]{:S(2)}, u32[]{:S(2)}) collective-permute-start(f32[4,1024]{1,0:T(4,128)S(1)} %constant_dynamic-update-slice_fusion.2.refs_0_), channel_id=1, source_target_pairs={{0,1},{1,0},{2,3},{3,2},{4,5},{5,4},{6,7},{7,6},{8,9},{9,8},{10,11... | collective-permute-start | bytes 49160 | tf_op jit(solution)/shard_map/ppermute | solution.py:290
  57.1 4.6 %collective-permute-start.9 = (f32[4,1024]{1,0:T(4,128)S(1)}, f32[4,1024]{1,0:T(4,128)S(1)}, u32[]{:S(2)}, u32[]{:S(2)}) collective-permute-start(f32[4,1024]{1,0:T(4,128)S(1)} %constant_dynamic-update-slice_fusion.2.refs_0_), channel_id=1, source_target_pairs={{0,2},{1,3},{2,0},{3,1},{4,6},{5,7},{6,4},{7,5},{8,10},{9,11},{10,... | collective-permute-start | bytes 49160 | tf_op jit(solution)/shard_map/ppermute | solution.py:290
  57.6 5.3 %collective-permute-start.10 = (f32[4,1024]{1,0:T(4,128)S(1)}, f32[4,1024]{1,0:T(4,128)S(1)}, u32[]{:S(2)}, u32[]{:S(2)}) collective-permute-start(f32[4,1024]{1,0:T(4,128)S(1)} %constant_dynamic-update-slice_fusion.2.refs_0_), channel_id=1, source_target_pairs={{0,3},{1,2},{2,1},{3,0},{4,7},{5,6},{6,5},{7,4},{8,11},{9,10},{10,... | collective-permute-start | bytes 49160 | tf_op jit(solution)/shard_map/ppermute | solution.py:290
  58.5 4.4 %collective-permute-start.11 = (f32[4,1024]{1,0:T(4,128)S(1)}, f32[4,1024]{1,0:T(4,128)S(1)}, u32[]{:S(2)}, u32[]{:S(2)}) collective-permute-start(f32[4,1024]{1,0:T(4,128)S(1)} %constant_dynamic-update-slice_fusion.2.refs_0_), channel_id=1, source_target_pairs={{0,4},{1,5},{2,6},{3,7},{4,0},{5,1},{6,2},{7,3},{8,12},{9,13},{10,... | collective-permute-start | bytes 49160 | tf_op jit(solution)/shard_map/ppermute | solution.py:290
  59.0 3.9 %collective-permute-start.12 = (f32[4,1024]{1,0:T(4,128)S(1)}, f32[4,1024]{1,0:T(4,128)S(1)}, u32[]{:S(2)}, u32[]{:S(2)}) collective-permute-start(f32[4,1024]{1,0:T(4,128)S(1)} %constant_dynamic-update-slice_fusion.2.refs_0_), channel_id=1, source_target_pairs={{0,5},{1,4},{2,7},{3,6},{4,1},{5,0},{6,3},{7,2},{8,13},{9,12},{10,... | collective-permute-start | bytes 49160 | tf_op jit(solution)/shard_map/ppermute | solution.py:290
  60.6 4.6 %collective-permute-start.13 = (f32[4,1024]{1,0:T(4,128)S(1)}, f32[4,1024]{1,0:T(4,128)S(1)}, u32[]{:S(2)}, u32[]{:S(2)}) collective-permute-start(f32[4,1024]{1,0:T(4,128)S(1)} %constant_dynamic-update-slice_fusion.2.refs_0_), channel_id=1, source_target_pairs={{0,6},{1,7},{2,4},{3,5},{4,2},{5,3},{6,0},{7,1},{8,14},{9,15},{10,... | collective-permute-start | bytes 49160 | tf_op jit(solution)/shard_map/ppermute | solution.py:290
  61.7 4.2 %collective-permute-start.14 = (f32[4,1024]{1,0:T(4,128)S(1)}, f32[4,1024]{1,0:T(4,128)S(1)}, u32[]{:S(2)}, u32[]{:S(2)}) collective-permute-start(f32[4,1024]{1,0:T(4,128)S(1)} %constant_dynamic-update-slice_fusion.2.refs_0_), channel_id=1, source_target_pairs={{0,7},{1,6},{2,5},{3,4},{4,3},{5,2},{6,1},{7,0},{8,15},{9,14},{10,... | collective-permute-start | bytes 49160 | tf_op jit(solution)/shard_map/ppermute | solution.py:290
  66.0 5.8 %collective-permute-start.15 = (f32[8,1024]{1,0:T(8,128)S(1)}, f32[8,1024]{1,0:T(8,128)S(1)}, u32[]{:S(2)}, u32[]{:S(2)}) collective-permute-start(f32[8,1024]{1,0:T(8,128)S(1)} %combine_stats.1.refs_0_), channel_id=1, source_target_pairs={{0,8},{8,16},{16,24},{24,0},{1,9},{9,17},{17,25},{25,1},{2,10},{10... | collective-permute-start | bytes 98312 | tf_op jit(solution)/shard_map/ppermute | solution.py:330
  67.7 5.3 %collective-permute-start.16 = (f32[8,1024]{1,0:T(8,128)S(1)}, f32[8,1024]{1,0:T(8,128)S(1)}, u32[]{:S(2)}, u32[]{:S(2)}) collective-permute-start(f32[8,1024]{1,0:T(8,128)S(1)} %combine_stats.1.refs_0_), channel_id=1, source_target_pairs={{0,16},{8,24},{16,0},{24,8},{1,17},{9,25},{17,1},{25,9},{2,18},{10... | collective-permute-start | bytes 98312 | tf_op jit(solution)/shard_map/ppermute | solution.py:330
  70.3 3.9 %collective-permute-start.17 = (f32[8,1024]{1,0:T(8,128)S(1)}, f32[8,1024]{1,0:T(8,128)S(1)}, u32[]{:S(2)}, u32[]{:S(2)}) collective-permute-start(f32[8,1024]{1,0:T(8,128)S(1)} %combine_stats.1.refs_0_), channel_id=1, source_target_pairs={{0,24},{8,0},{16,8},{24,16},{1,25},{9,1},{17,9},{25,17},{2,26},{10... | collective-permute-start | bytes 98312 | tf_op jit(solution)/shard_map/ppermute | solution.py:330

commit v2 on v1

v2 whole, which is shorter than its diff:
```python
import functools

import jax
import jax.numpy as jnp
from jax import lax
from jax.experimental import pallas as pl
from jax.experimental.pallas import tpu as pltpu
from jax.sharding import PartitionSpec as P

eps_norm = 1e-05
live_cap = 128
extra = 16
column_unit = 4000
lowest = -1e30
ahead = 3
places = (0, 1, 2, 4, 3, 5, 6, 7)
vmem_bytes = 10 * 1024 * 1024
f32 = jnp.float32


def prepare_kernel(
    lengths_in, hidden_in, gain_in, targets_in, out_ref, lengths_ref, hidden_ref, gain_ref, targets_ref, sems
):
    pairs = (
        (hidden_in, hidden_ref),
        (lengths_in, lengths_ref),
        (targets_in, targets_ref),
        (gain_in, gain_ref),
    )
    copies = [pltpu.make_async_copy(a, b, sems.at[i]) for i, (a, b) in enumerate(pairs)]
    for copy in copies:
        copy.start()
    for copy in copies:
        copy.wait()
    rows, depth = hidden_ref.shape
    seq_count = lengths_ref.shape[0]
    seq_len = rows // seq_count
    values = hidden_ref[...].astype(f32)
    inverse_rms = lax.rsqrt(jnp.mean(values * values, axis=1, keepdims=True) + eps_norm)
    normed = (values * inverse_rms * gain_ref[...]).astype(jnp.bfloat16)
    row = lax.broadcasted_iota(jnp.int32, (1, rows), 1)
    sublane = lax.broadcasted_iota(jnp.int32, (extra, live_cap), 0)
    lane = lax.broadcasted_iota(jnp.int32, (extra, live_cap), 1)
    place = jnp.full((1, rows), -1, jnp.int32)
    meta = jnp.zeros((extra, live_cap), jnp.int32)
    start = jnp.int32(0)
    for request in range(seq_count):
        length = lengths_ref[request]
        first = request * seq_len
        place = jnp.where((row >= first) & (row < first + length), row - first + start, place)
        meta = jnp.where(lane == request, start, meta)
        meta = jnp.where(lane == seq_count + request, length, meta)
        start = start + length
    chosen = lax.broadcasted_iota(jnp.int32, (live_cap, rows), 0) == place
    selector = chosen.astype(f32).astype(jnp.bfloat16)
    kept = jnp.dot(selector, normed, preferred_element_type=f32)
    for first in range(0, depth, 128):
        out_ref[first : first + 128, :] = kept[:, first : first + 128].T.astype(jnp.bfloat16)
    target = jnp.sum(jnp.where(chosen, targets_ref[...], 0), axis=1, keepdims=True)
    target = jnp.broadcast_to(target.astype(f32), (live_cap, 128)).T[:extra].astype(jnp.int32)
    meta = jnp.where(sublane == 0, target >> 8, meta)
    meta = jnp.where(sublane == 1, target & 255, meta)
    out_ref[depth:, :] = meta.astype(f32).astype(jnp.bfloat16)


def prepare(hidden_states, norm_gain, targets, lengths):
    rows, depth = hidden_states.shape
    return pl.pallas_call(
        prepare_kernel,
        out_shape=jax.ShapeDtypeStruct((depth + extra, live_cap), jnp.bfloat16),
        in_specs=[pl.BlockSpec(memory_space=pltpu.HBM)] * 4,
        out_specs=pl.BlockSpec(memory_space=pltpu.VMEM),
        scratch_shapes=[
            pltpu.SMEM(lengths.shape, jnp.int32),
            pltpu.VMEM((rows, depth), jnp.bfloat16),
            pltpu.VMEM((1, depth), f32),
            pltpu.VMEM((1, rows), jnp.int32),
            pltpu.SemaphoreType.DMA((4,)),
        ],
        compiler_params=pltpu.CompilerParams(vmem_limit_bytes=6 * vmem_bytes),
        name="prepare_rows",
    )(lengths, hidden_states, norm_gain.reshape(1, depth), targets.reshape(1, rows))


def stats_kernel(block_count, vocab_cols, steps, halves, piece_rows, mode, *refs):
    blocks = refs[:block_count]
    weight_ref = refs[block_count]
    if mode == "load":
        weight_in, weight_ref, sems = weight_ref, refs[block_count + 3], refs[-1]
        refs = refs[: block_count + 3] + refs[block_count + 4 : -1]
    out_ref, meta_ref = refs[-10:-8]
    rows_ref, even_ref, odd_ref, peak_ref, total_ref, spread_ref, picked_ref, offset_ref = refs[-8:]
    logits_refs = (even_ref, odd_ref)
    depth = weight_ref.shape[1]
    rows = block_count * live_cap
    part_vocab = even_ref.shape[0]
    tile_vocab = part_vocab * halves
    units = rows // piece_rows * halves
    vocab_start = lax.axis_index("vocab") * vocab_cols
    last_valid = vocab_cols - (steps - 1) * tile_vocab

    def arrival(index):
        own = pl.ds(pl.multiple_of(index * part_vocab, 16), part_vocab)
        return pltpu.make_async_copy(weight_in.at[own], weight_ref.at[own], sems.at[index])

    def begin():
        if mode == "load":
            for index in range(ahead):
                arrival(index).start(priority=index % 2)
        for place, block in enumerate(blocks):
            rows_ref[:, pl.ds(place * live_cap, live_cap)] = block[...]
        peak_ref[...] = jnp.full(peak_ref.shape, lowest, f32)
        total_ref[...] = jnp.zeros(total_ref.shape, f32)
        spread_ref[...] = jnp.zeros(spread_ref.shape, f32)
        picked_ref[...] = jnp.zeros(picked_ref.shape, f32)
        if steps > 1:
            logits_refs[(units - 1) % 2][...] = jnp.full(even_ref.shape, lowest, f32)
        digits = rows_ref[depth:, :].astype(f32)
        target = (digits[0:1] * 256.0 + digits[1:2]).astype(jnp.int32) - vocab_start
        target = jnp.where((target >= 0) & (target < vocab_cols), target, 2 * steps * tile_vocab)
        offset_ref[...] = target - lax.broadcasted_iota(jnp.int32, (8, rows), 0)
        meta_ref[...] = digits[2:3]

    def absorb(unit, tile):
        logits_ref = logits_refs[unit % 2]
        piece, half = divmod(unit, halves)
        base = half * part_vocab
        sublane = lax.broadcasted_iota(jnp.int32, (8, 128), 0)
        for part in range(piece_rows // 128):
            own = pl.ds(piece * piece_rows + part * 128, 128)

            def load(group):
                values = logits_ref[pl.ds(group * 8, 8), pl.ds(part * 128, 128)]
                if base + (group + 1) * 8 > last_valid:
                    left = vocab_cols - tile * tile_vocab - base - group * 8
                    values = jnp.where(sublane < left, values, lowest)
                return values

            groups = part_vocab // 8
            ways = 4
            tops = [load(group) for group in range(ways)]
            for group in range(ways, groups):
                tops[group % ways] = jnp.maximum(tops[group % ways], load(group))
            before = peak_ref[:, own]
            peak = functools.reduce(jnp.maximum, tops, before)
            change = before - peak
            factor = jnp.exp(change)
            total = total_ref[:, own]
            spread = factor * (spread_ref[:, own] + change * total)
            total = total * factor
            picked = picked_ref[:, own]
            offset = offset_ref[:, own]
            totals = [total] + [jnp.zeros_like(total)] * (ways - 1)
            spreads = [spread] + [jnp.zeros_like(total)] * (ways - 1)
            for group in range(groups):
                values = load(group)
                shifted = values - peak
                exponent = jnp.exp(shifted)
                totals[group % ways] = totals[group % ways] + exponent
                spreads[group % ways] = spreads[group % ways] + exponent * shifted
                picked = jnp.where(offset == tile * tile_vocab + base + group * 8, values, picked)
            peak_ref[:, own] = peak
            total_ref[:, own] = (totals[0] + totals[1]) + (totals[2] + totals[3])
            spread_ref[:, own] = (spreads[0] + spreads[1]) + (spreads[2] + spreads[3])
            picked_ref[:, own] = picked

    def advance(step, first):
        for unit in range(units):
            piece, half = divmod(unit, halves)
            at = first + half * part_vocab
            if steps > 1:
                at = pl.multiple_of(at, 16)
            if mode == "load" and piece == 0:
                index = step * halves + half
                arrival(index).wait()

                @pl.when(index + ahead < steps * halves)
                def _():
                    arrival(index + ahead).start(priority=(half + ahead) % 2)

            logits_refs[unit % 2][...] = jnp.dot(
                weight_ref[pl.ds(at, part_vocab), :],
                rows_ref[:depth, pl.ds(piece * piece_rows, piece_rows)],
                preferred_element_type=f32,
            )
            if unit == 0 and steps > 1:
                absorb(units - 1, step - 1)
            if unit > 0:
                absorb(unit - 1, step)

    def finish():
        absorb(units - 1, steps - 1)
        peak = peak_ref[...]
        total = total_ref[...]
        top = jnp.max(peak, axis=0, keepdims=True)
        change = peak - top
        factor = jnp.exp(change)
        out_ref[0:1, :] = top
        out_ref[1:2, :] = jnp.sum(total * factor, axis=0, keepdims=True)
        out_ref[2:3, :] = jnp.sum(factor * (spread_ref[...] + change * total), axis=0, keepdims=True)
        out_ref[3:4, :] = jnp.sum(picked_ref[...], axis=0, keepdims=True)

    if mode != "stream" and steps == 1:
        begin()
        advance(0, 0)
        finish()
    elif mode != "stream":
        begin()

        @pl.loop(0, steps)
        def _(step):
            advance(step, step * tile_vocab)

        finish()
    else:
        step = pl.program_id(0)
        pl.when(step == 0)(begin)
        advance(step, 0)
        pl.when(step == steps - 1)(finish)


def block_stats(blocks, weight_rows, mode, part_vocab=400, halves=2, piece_rows=256):
    count = len(blocks)
    rows = count * live_cap
    vocab_cols, depth = weight_rows.shape
    tile_vocab = part_vocab * halves
    steps = -(-vocab_cols // tile_vocab)
    whole = pl.BlockSpec(memory_space=pltpu.VMEM)
    shapes = (jax.ShapeDtypeStruct((4, rows), f32), jax.ShapeDtypeStruct((1, rows), f32))
    scratch = [
        pltpu.VMEM((depth + extra, rows), jnp.bfloat16),
        pltpu.VMEM((part_vocab, piece_rows), f32),
        pltpu.VMEM((part_vocab, piece_rows), f32),
        pltpu.VMEM((8, rows), f32),
        pltpu.VMEM((8, rows), f32),
        pltpu.VMEM((8, rows), f32),
        pltpu.VMEM((8, rows), f32),
        pltpu.VMEM((8, rows), jnp.int32),
    ]
    limit = vmem_bytes
    if mode == "stream":
        limit = 4 * vmem_bytes
        specs = dict(
            grid=(steps,),
            in_specs=[pl.BlockSpec((depth + extra, live_cap), lambda step: (0, 0))] * count
            + [pl.BlockSpec((tile_vocab, depth), lambda step: (step, 0))],
            out_specs=(
                pl.BlockSpec((4, rows), lambda step: (0, 0)),
                pl.BlockSpec((1, rows), lambda step: (0, 0)),
            ),
        )
    elif mode == "load":
        limit = 3 * vmem_bytes
        specs = dict(
            in_specs=[whole] * count + [pl.BlockSpec(memory_space=pltpu.HBM)], out_specs=(whole, whole, whole)
        )
        shapes = shapes + (jax.ShapeDtypeStruct(weight_rows.shape, weight_rows.dtype),)
        scratch = scratch + [pltpu.SemaphoreType.DMA((vocab_cols // part_vocab,))]
    else:
        specs = dict(in_specs=[whole] * (count + 1), out_specs=(whole, whole))
    return pl.pallas_call(
        functools.partial(stats_kernel, count, vocab_cols, steps, halves, piece_rows, mode),
        out_shape=shapes,
        scratch_shapes=scratch,
        compiler_params=pltpu.CompilerParams(vmem_limit_bytes=limit),
        cost_estimate=pl.CostEstimate(
            flops=2 * rows * depth * vocab_cols,
            bytes_accessed=2 * depth * (vocab_cols if mode == "load" else rows),
            transcendentals=rows * vocab_cols,
        ),
        name="row_stats",
        **specs,
    )(*blocks, weight_rows)


def merge(parts):
    top = functools.reduce(jnp.maximum, [part[0:1] for part in parts])
    total = jnp.zeros_like(top)
    spread = jnp.zeros_like(top)
    picked = jnp.zeros_like(top)
    for part in parts:
        change = part[0:1] - top
        factor = jnp.exp(change)
        total = total + part[1:2] * factor
        spread = spread + factor * (part[2:3] + change * part[1:2])
        picked = picked + part[3:4]
    return top, total, spread, picked


def merge_kernel(there_of, mine_ref, other_ref, out_ref):
    for place, there in enumerate(there_of):
        own = pl.ds(place * live_cap, live_cap)
        there = pl.ds(there * live_cap, live_cap)
        for row, value in enumerate(merge((mine_ref[:, own], other_ref[:, there]))):
            out_ref[row : row + 1, own] = value


def merge_pair(there_of, mine, other):
    return pl.pallas_call(
        functools.partial(merge_kernel, there_of),
        out_shape=jax.ShapeDtypeStruct(mine.shape, f32),
        in_specs=[pl.BlockSpec(memory_space=pltpu.VMEM)] * 2,
        out_specs=pl.BlockSpec(memory_space=pltpu.VMEM),
        compiler_params=pltpu.CompilerParams(vmem_limit_bytes=vmem_bytes),
        name="merge_stats",
    )(mine, other)


def result_kernel(order, *refs):
    peers = refs[: len(order)]
    meta_ref, out_ref = refs[len(order) :]
    for place in range(len(order[0])):
        own = pl.ds(place * live_cap, live_cap)
        top, total, spread, picked = merge(
            [peer[:, pl.ds(order[j][place] * live_cap, live_cap)] for j, peer in enumerate(peers)]
        )
        log_total = jnp.log(total)
        out_ref[0:1, own] = picked - top - log_total
        out_ref[1:2, own] = log_total - spread / total
        out_ref[2:3, own] = meta_ref[:, own]
        out_ref[3:4, own] = jnp.zeros((1, live_cap), f32)


def finish_rows(peers, order, meta):
    rows = meta.shape[1]
    return pl.pallas_call(
        functools.partial(result_kernel, order),
        out_shape=jax.ShapeDtypeStruct((4, rows), f32),
        in_specs=[pl.BlockSpec(memory_space=pltpu.VMEM)] * (len(peers) + 1),
        out_specs=pl.BlockSpec(memory_space=pltpu.VMEM),
        compiler_params=pltpu.CompilerParams(vmem_limit_bytes=vmem_bytes),
        name="finish_rows",
    )(*peers, meta)


def pick_kernel(vocab_count, paired, seq_len, slot_ref, near_ref, far_ref, logprob_ref, entropy_ref, *found_refs):
    seq_count = slot_ref.shape[0]
    req = lax.axis_index("req")
    vocab = lax.axis_index("vocab")
    half = near_ref.shape[0] // 4
    lane = lax.broadcasted_iota(jnp.int32, (seq_count, 128), 1)
    sublane = lax.broadcasted_iota(jnp.int32, (seq_count, 128), 0)
    within_all = jnp.zeros((seq_count, 128), jnp.int32)
    for request in range(seq_count):
        slot = slot_ref[request]
        owner = slot // seq_count
        owner_req = owner // vocab_count
        place = owner - owner_req * vocab_count
        if paired:
            block = place ^ vocab
            place = jnp.int32(0)
            for k in range(vocab_count):
                place = jnp.where(block == k, places[k], place)
        columns = pl.ds(pl.multiple_of(place * live_cap, live_cap), live_cap)
        apart = owner_req ^ req
        chosen = jnp.zeros((4, live_cap), f32)
        for j in range(half):
            chosen = jnp.where(apart == j, near_ref[4 * j : 4 * j + 4, columns], chosen)
            chosen = jnp.where(apart == j + half, far_ref[4 * j : 4 * j + 4, columns], chosen)
        for row, found_ref in enumerate(found_refs):
            found_ref[request : request + 1, :] = chosen[row : row + 1]
        within_all = jnp.where(sublane == request, slot - owner * seq_count, within_all)
    meta = found_refs[2][...]
    start = jnp.sum(jnp.where(lane == within_all, meta, 0.0), axis=1, keepdims=True).astype(jnp.int32)
    length = jnp.sum(jnp.where(lane == seq_count + within_all, meta, 0.0), axis=1, keepdims=True).astype(jnp.int32)
    index = jnp.minimum(start + lane, live_cap - 1)
    for found_ref, result_ref in zip(found_refs, (logprob_ref, entropy_ref)):
        found = jnp.take_along_axis(found_ref[...], index, axis=1, mode="promise_in_bounds")
        result_ref[...] = jnp.where(lane < length, found, 0.0)[:, :seq_len]


def pick(slot_of, near, far, vocab_count, paired, seq_len):
    seq_count = slot_of.shape[0]
    shape = jax.ShapeDtypeStruct((seq_count, seq_len), f32)
    whole = pl.BlockSpec(memory_space=pltpu.VMEM)
    return pl.pallas_call(
        functools.partial(pick_kernel, vocab_count, paired, seq_len),
        out_shape=(shape, shape),
        in_specs=[pl.BlockSpec(memory_space=pltpu.SMEM), whole, whole],
        out_specs=(whole, whole),
        scratch_shapes=[pltpu.VMEM((seq_count, live_cap), f32)] * 3,
        compiler_params=pltpu.CompilerParams(vmem_limit_bytes=vmem_bytes),
        name="pick_requests",
    )(slot_of, near, far)


def there_of(mask):
    blocks = sorted(range(len(places)), key=lambda k: places[k])
    return [places[k ^ mask] for k in blocks]


def swap(array, mask, count):
    return lax.ppermute(array, "vocab", [(i, i ^ mask) for i in range(count)])


def local(vocab_count, req_count, hidden_states, norm_gain, head_weight, targets, lengths, slot_of):
    seq_len = hidden_states.shape[0] // lengths.shape[0]
    own = prepare(hidden_states, norm_gain, targets, lengths)
    weight_rows = head_weight.T
    paired = vocab_count == 8 and head_weight.shape[1] % column_unit == 0
    if paired:
        x_same = swap(own, 2, vocab_count)
        y_same = swap(own, 4, vocab_count)
        core = swap(own, 1, vocab_count)
        *first, weight_rows = block_stats((own, core), weight_rows, "load")
        x_same, y_same, weight_rows = lax.optimization_barrier((x_same, y_same, weight_rows))
        half = own.shape[0] // 32 * 16
        diagonal_low = swap(x_same[:half], 4, vocab_count)
        diagonal_high = swap(y_same[half:], 2, vocab_count)
        x_other = swap(x_same, 1, vocab_count)
        y_other = swap(y_same, 1, vocab_count)
        second = block_stats((x_same, y_same), weight_rows, "resident", 800, 5)
        diagonal_low, diagonal_high, *second = lax.optimization_barrier((diagonal_low, diagonal_high, *second))
        diagonal = jnp.concatenate((diagonal_low, diagonal_high), axis=0)
        diagonal_other = swap(diagonal, 1, vocab_count)
        third = block_stats((x_other, y_other, diagonal, diagonal_other), weight_rows, "resident", 400, 2, 512)
        calls = (first, second, third)
    else:
        gathered = lax.all_gather(own, "vocab", axis=0)
        calls = [
            block_stats([gathered[k] for k in range(at, min(at + 4, vocab_count))], weight_rows, "stream")
            for at in range(0, vocab_count, 4)
        ]
    stats = jnp.concatenate([call[0] for call in calls], axis=1)
    meta = jnp.concatenate([call[1] for call in calls], axis=1)
    if paired:
        for mask in (1, 2):
            stats = merge_pair(there_of(mask), stats, swap(stats, mask, vocab_count))
        peers = (stats, swap(stats, 4, vocab_count))
        order = [there_of(0), there_of(4)]
    else:
        everyone = lax.all_gather(stats, "vocab", axis=0)
        peers = [everyone[j] for j in range(vocab_count)]
        order = [list(range(vocab_count))] * vocab_count
    near = finish_rows(peers, order, meta)
    mask = 1
    while True:
        far = lax.ppermute(near, "req", [(i, i ^ mask) for i in range(req_count)])
        mask = 2 * mask
        if mask == req_count:
            break
        near = jnp.concatenate((near, far), axis=0)
    return pick(slot_of, near, far, vocab_count, paired, seq_len)


def solution(mesh):
    in_specs = (
        P(("req", "vocab"), None),
        P(),
        P(None, "vocab"),
        P(("req", "vocab")),
        P(("req", "vocab")),
        P(("req", "vocab")),
    )
    out_specs = (P(("req", "vocab"), None), P(("req", "vocab"), None))
    body = functools.partial(local, mesh.shape["vocab"], mesh.shape["req"])
    return jax.shard_map(body, mesh=mesh, in_specs=in_specs, out_specs=out_specs, check_vma=False)
```

time: 76.1 us -> 64.4 us (0.85)
  starting transfers between devices: 20.4 us -> 14.9 us
  waiting for transfers between devices: 16 us -> 13.1 us
  local copies, waits for them, and re-layouts: 3.27 us -> 1.19 us
  Pallas kernels: 35.2 us -> 34.2 us
    ppermute x15 -> x11, waiting for transfers between devices: 13.5 us -> 8.74 us  [swap(): return lax.ppermute(array, 'vocab', [(i, i ^ mask) for i in range(count)])]
    ppermute x15 -> x11, starting transfers between devices: 14.8 us -> 10.6 us  [swap(): return lax.ppermute(array, 'vocab', [(i, i ^ mask) for i in range(count)])]
    pallas_call x5 -> x7, Pallas kernels: 34 us -> 31.6 us  [the longest x3 30 us: block_stats(): pl.pallas_call(functools.partial(stats_kernel, count, vocab_cols, steps,...]
    unnamed x13 -> x7, local copies, waits for them, and re-layouts: 3.19 us -> 1.11 us
    ppermute x3 -> x2, waiting for transfers between devices: 2.57 us -> 4.4 us  [local(): far = lax.ppermute(near, 'req', [(i, i ^ mask) for i in range(req_count)])]
    pallas_call x1, Pallas kernels: 1.21 us -> 2.66 us  [prepare(): pl.pallas_call(prepare_kernel, out_shape=jax.ShapeDtypeStruct((depth + ex...]
    ppermute x3 -> x2, starting transfers between devices: 5.56 us -> 4.28 us  [local(): far = lax.ppermute(near, 'req', [(i, i ^ mask) for i in range(req_count)])]
  transfers between devices with their start and end apart: 18 -> 13, of which waited for: 6 -> 8; matrix products, arithmetic and copies ran while one was open for 0% -> 0% of each run, Pallas kernels for 30% -> 28%
where the time goes in v2:
time: 64.4 us; the launch traced here: 64.2 us
  Pallas kernels  34.2 us (53%)
  starting transfers between devices  14.9 us (23%)
  waiting for transfers between devices  13.1 us (20%)
  local copies, waits for them, and re-layouts  1.19 us (2%)
  between operations  0.77 us (1%)
    pallas_call x3, Pallas kernels, block_stats(): pl.pallas_call(functools.partial(stats_kernel, count, vocab_cols, steps,...  30 us
    ppermute x11, starting transfers between devices, swap(): return lax.ppermute(array, 'vocab', [(i, i ^ mask) for i in range(count)])  10.6 us
    ppermute x11, waiting for transfers between devices, swap(): return lax.ppermute(array, 'vocab', [(i, i ^ mask) for i in range(count)])  8.74 us
    ppermute x2, waiting for transfers between devices, local(): far = lax.ppermute(near, 'req', [(i, i ^ mask) for i in range(req_count)])  4.4 us
    ppermute x2, starting transfers between devices, local(): far = lax.ppermute(near, 'req', [(i, i ^ mask) for i in range(req_count)])  4.28 us
    pallas_call x1, Pallas kernels, prepare(): pl.pallas_call(prepare_kernel, out_shape=jax.ShapeDtypeStruct((depth + ex...  2.66 us
    pallas_call x1, Pallas kernels, pick(): pl.pallas_call(functools.partial(pick_kernel, vocab_count, paired, seq_le...  1.46 us
  transfers between devices with their start and end apart: 13, of which 8 were waited for; matrix products, arithmetic and copies ran while one was open for 0% of the time, Pallas kernels for 28%

profile of v2, /device:TPU:0, one launch (start us, length us, event | category | flops | bytes accessed | tf_op | source)
XLA Modules:
  0.0 64.2 jit_solution(10409978293070358693)
XLA Ops:
  0.6 2.7 %prepare_rows.1.refs_0_ = bf16[2064,128]{1,0:T(8,128)(2,1)} custom-call(s32[8]{0:T(128)} %lengths_in.1, bf16[192,2048]{1,0:T(8,128)(2,1)} %hidden_in.1, f32[1,2048]{1,0:T(1,128)} %bitcast.4, s32[1,192]{1,0:T(1,128)} %bitcast.5), custom_call_target="tpu_custom_call" | custom-call | tf_op jit(solution)/shard_map/prepare_rows/pallas_call | solution.py:68
  3.3 0.5 collective-permute-start
  3.8 2.6 %collective-permute-start.1 = (bf16[2064,128]{1,0:T(8,128)(2,1)}, bf16[2064,128]{1,0:T(8,128)(2,1)S(1)}, u32[]{:S(2)}, u32[]{:S(2)}) collective-permute-start(bf16[2064,128]{1,0:T(8,128)(2,1)} %prepare_rows.1.refs_0_), channel_id=1, source_target_pairs={{0,2},{1,3},{2,0},{3,1},{4,6},{5,7},{6,4},{7,5},{8,10},{9,11},{10,... | collective-permute-start | bytes 1585160 | tf_op jit(solution)/shard_map/ppermute | solution.py:393
  6.4 1.5 %collective-permute-start.2 = (bf16[2064,128]{1,0:T(8,128)(2,1)}, bf16[2064,128]{1,0:T(8,128)(2,1)S(1)}, u32[]{:S(2)}, u32[]{:S(2)}) collective-permute-start(bf16[2064,128]{1,0:T(8,128)(2,1)} %prepare_rows.1.refs_0_), channel_id=1, source_target_pairs={{0,4},{1,5},{2,6},{3,7},{4,0},{5,1},{6,2},{7,3},{8,12},{9,13},{10,... | collective-permute-start | bytes 1585160 | tf_op jit(solution)/shard_map/ppermute | solution.py:393
  7.9 0.0 collective-permute-done.refs_1_
  7.9 1.1 %copy-done = bf16[2064,128]{1,0:T(8,128)(2,1)S(1)} copy-done((bf16[2064,128]{1,0:T(8,128)(2,1)S(1)}, bf16[2064,128]{1,0:T(8,128)(2,1)}, u32[]{:S(2)}) %copy-start) | copy-done | bytes 528408
  9.0 12.7 %row_stats.3 = (f32[4,256]{1,0:T(4,128)S(1)}, f32[1,256]{1,0:T(1,128)S(1)}, bf16[4000,2048]{1,0:T(8,128)(2,1)S(1)}) custom-call(bf16[2064,128]{1,0:T(8,128)(2,1)S(1)} %copy-done, bf16[2064,128]{1,0:T(8,128)(2,1)S(1)} %collective-permute-done.refs_1_, bf16[4000,2048]{1,0:T(8,128)(2,1)} %bitcast.3), custom_call_target="tpu_custom_call" | custom-call | flops 4194304000 | bytes 16384000 | tf_op jit(solution)/shard_map/row_stats/pallas_call | solution.py:261
  21.7 0.0 collective-permute-done.2.refs_1_
  21.7 0.1 collective-permute-start.5
  21.8 0.6 collective-permute-start.6
  22.4 0.5 collective-permute-start.3
  22.9 1.5 %collective-permute-start.4 = (bf16[1040,128]{1,0:T(8,128)(2,1)S(1)}, bf16[1040,128]{1,0:T(8,128)(2,1)S(1)}, u32[]{:S(2)}, u32[]{:S(2)}) collective-permute-start(bf16[1040,128]{1,0:T(8,128)(2,1)S(1)} %slice.7), channel_id=1, source_target_pairs={{0,2},{1,3},{2,0},{3,1},{4,6},{5,7},{6,4},{7,5},{8,10},{9,11},{10,... | collective-permute-start | bytes 798728 | tf_op jit(solution)/shard_map/ppermute | solution.py:393
  24.4 5.4 %row_stats.4 = (f32[4,256]{1,0:T(4,128)S(1)}, f32[1,256]{1,0:T(1,128)S(1)}) custom-call(bf16[2064,128]{1,0:T(8,128)(2,1)S(1)} %collective-permute-done.1.refs_0_, bf16[2064,128]{1,0:T(8,128)(2,1)S(1)} %collective-permute-done.2.refs_1_, bf16[4000,2048]{1,0:T(8,128)(2,1)S(1)} %get-tuple-element.20.refs_2_.refs_4_), custom_call_target="tpu_custom_call" | custom-call | flops 4194304000 | bytes 1048576 | tf_op jit(solution)/shard_map/row_stats/pallas_call | solution.py:261
  29.8 0.0 copy-start.1
  29.8 0.9 %collective-permute-done.3 = bf16[1024,128]{1,0:T(8,128)(2,1)S(1)} collective-permute-done((bf16[1024,128]{1,0:T(8,128)(2,1)S(1)}, bf16[1024,128]{1,0:T(8,128)(2,1)S(1)}, u32[]{:S(2)}, u32[]{:S(2)}) %collective-permute-start.3) | collective-permute-done | bytes 262176 | tf_op jit(solution)/shard_map/ppermute | solution.py:393
  30.7 0.4 collective-permute-done.4
  31.1 0.1 collective-permute-start.7
  31.2 0.0 collective-permute-done.5.refs_0_
  31.3 1.9 %collective-permute-done.7.refs_3_ = bf16[2064,128]{1,0:T(8,128)(2,1)S(1)} collective-permute-done((bf16[2064,128]{1,0:T(8,128)(2,1)S(1)}, bf16[2064,128]{1,0:T(8,128)(2,1)S(1)}, u32[]{:S(2)}, u32[]{:S(2)}) %collective-permute-start.7) | collective-permute-done | bytes 528416 | tf_op jit(solution)/shard_map/ppermute | solution.py:393
  33.1 11.9 %row_stats.5 = (f32[4,512]{1,0:T(4,128)S(1)}, f32[1,512]{1,0:T(1,128)S(1)}) custom-call(bf16[2064,128]{1,0:T(8,128)(2,1)S(1)} %collective-permute-done.5.refs_0_, bf16[2064,128]{1,0:T(8,128)(2,1)S(1)} %collective-permute-done.6.refs_1_, bf16[2064,128]{1,0:T(8,128)(2,1)S(1)} %constant_dynamic-update-slice_fusion.refs_2_, ...), custom_call_target="tpu_custom_call" | custom-call | flops 8388608000 | bytes 2097152 | tf_op jit(solution)/shard_map/row_stats/pallas_call | solution.py:261
  45.0 0.2 collective-permute-start.8
  45.2 1.1 %collective-permute-done.8.other_ref = f32[4,1024]{1,0:T(4,128)S(1)} collective-permute-done((f32[4,1024]{1,0:T(4,128)S(1)}, f32[4,1024]{1,0:T(4,128)S(1)}, u32[]{:S(2)}, u32[]{:S(2)}) %collective-permute-start.8) | collective-permute-done | bytes 16416 | tf_op jit(solution)/shard_map/ppermute | solution.py:393
  46.3 1.6 %collective-permute-start.9 = (f32[4,1024]{1,0:T(4,128)S(1)}, f32[4,1024]{1,0:T(4,128)S(1)}, u32[]{:S(2)}, u32[]{:S(2)}) collective-permute-start(f32[4,1024]{1,0:T(4,128)S(1)} %merge_stats.2.mine_ref), channel_id=1, source_target_pairs={{0,2},{1,3},{2,0},{3,1},{4,6},{5,7},{6,4},{7,5},{8,10},{9,11},{10,... | collective-permute-start | bytes 49160 | tf_op jit(solution)/shard_map/ppermute | solution.py:393
  47.9 2.2 %collective-permute-done.9.other_ref = f32[4,1024]{1,0:T(4,128)S(1)} collective-permute-done((f32[4,1024]{1,0:T(4,128)S(1)}, f32[4,1024]{1,0:T(4,128)S(1)}, u32[]{:S(2)}, u32[]{:S(2)}) %collective-permute-start.9) | collective-permute-done | bytes 16416 | tf_op jit(solution)/shard_map/ppermute | solution.py:393
  50.2 1.5 %collective-permute-start.10 = (f32[4,1024]{1,0:T(4,128)S(1)}, f32[4,1024]{1,0:T(4,128)S(1)}, u32[]{:S(2)}, u32[]{:S(2)}) collective-permute-start(f32[4,1024]{1,0:T(4,128)S(1)} %merge_stats.3.refs_0_), channel_id=1, source_target_pairs={{0,4},{1,5},{2,6},{3,7},{4,0},{5,1},{6,2},{7,3},{8,12},{9,13},{10,... | collective-permute-start | bytes 49160 | tf_op jit(solution)/shard_map/ppermute | solution.py:393
  51.7 2.3 %collective-permute-done.10.refs_1_ = f32[4,1024]{1,0:T(4,128)S(1)} collective-permute-done((f32[4,1024]{1,0:T(4,128)S(1)}, f32[4,1024]{1,0:T(4,128)S(1)}, u32[]{:S(2)}, u32[]{:S(2)}) %collective-permute-start.10) | collective-permute-done | bytes 16416 | tf_op jit(solution)/shard_map/ppermute | solution.py:393
  54.0 0.1 finish_rows.1
  54.0 1.6 %collective-permute-start.11 = (f32[4,1024]{1,0:T(4,128)S(1)}, f32[4,1024]{1,0:T(4,128)S(1)}, u32[]{:S(2)}, u32[]{:S(2)}) collective-permute-start(f32[4,1024]{1,0:T(4,128)S(1)} %finish_rows.1), channel_id=1, source_target_pairs={{0,8},{8,0},{16,24},{24,16},{1,9},{9,1},{17,25},{25,17},{2,10},{10... | collective-permute-start | bytes 49160 | tf_op jit(solution)/shard_map/ppermute | solution.py:438
  55.7 2.2 %collective-permute-done.11 = f32[4,1024]{1,0:T(4,128)S(1)} collective-permute-done((f32[4,1024]{1,0:T(4,128)S(1)}, f32[4,1024]{1,0:T(4,128)S(1)}, u32[]{:S(2)}, u32[]{:S(2)}) %collective-permute-start.11) | collective-permute-done | bytes 16416 | tf_op jit(solution)/shard_map/ppermute | solution.py:438
  57.9 2.6 %collective-permute-start.12 = (f32[8,1024]{1,0:T(8,128)S(1)}, f32[8,1024]{1,0:T(8,128)S(1)}, u32[]{:S(2)}, u32[]{:S(2)}) collective-permute-start(f32[8,1024]{1,0:T(8,128)S(1)} %pad_maximum_fusion.near_ref), channel_id=1, source_target_pairs={{0,16},{8,24},{16,0},{24,8},{1,17},{9,25},{17,1},{25,9},{2,18},{10... | collective-permute-start | bytes 98312 | tf_op jit(solution)/shard_map/ppermute | solution.py:438
  60.5 2.2 %collective-permute-done.12.far_ref = f32[8,1024]{1,0:T(8,128)S(1)} collective-permute-done((f32[8,1024]{1,0:T(8,128)S(1)}, f32[8,1024]{1,0:T(8,128)S(1)}, u32[]{:S(2)}, u32[]{:S(2)}) %collective-permute-start.12) | collective-permute-done | bytes 32800 | tf_op jit(solution)/shard_map/ppermute | solution.py:438
  62.7 1.5 %pick_requests.1 = (f32[8,24]{1,0:T(8,128)}, f32[8,24]{1,0:T(8,128)}) custom-call(s32[8]{0:T(128)S(1)} %copy-done.1, f32[8,1024]{1,0:T(8,128)S(1)} %pad_maximum_fusion.near_ref, f32[8,1024]{1,0:T(8,128)S(1)} %collective-permute-done.12.far_ref), custom_call_target="tpu_custom_call" | custom-call | tf_op jit(solution)/shard_map/pick_requests/pallas_call | solution.py:376
  (15 shorter events, 0.2 us)
Async XLA Ops:
  3.3 4.6 %collective-permute-start = (bf16[2064,128]{1,0:T(8,128)(2,1)}, bf16[2064,128]{1,0:T(8,128)(2,1)S(1)}, u32[]{:S(2)}, u32[]{:S(2)}) collective-permute-start(bf16[2064,128]{1,0:T(8,128)(2,1)} %prepare_rows.1.refs_0_), channel_id=1, source_target_pairs={{0,1},{1,0},{2,3},{3,2},{4,5},{5,4},{6,7},{7,6},{8,9},{9,8},{10,11... | collective-permute-start | bytes 1585160 | tf_op jit(solution)/shard_map/ppermute | solution.py:393
  3.8 17.9 %collective-permute-start.1 = (bf16[2064,128]{1,0:T(8,128)(2,1)}, bf16[2064,128]{1,0:T(8,128)(2,1)S(1)}, u32[]{:S(2)}, u32[]{:S(2)}) collective-permute-start(bf16[2064,128]{1,0:T(8,128)(2,1)} %prepare_rows.1.refs_0_), channel_id=1, source_target_pairs={{0,2},{1,3},{2,0},{3,1},{4,6},{5,7},{6,4},{7,5},{8,10},{9,11},{10,... | collective-permute-start | bytes 1585160 | tf_op jit(solution)/shard_map/ppermute | solution.py:393
  6.4 15.3 %collective-permute-start.2 = (bf16[2064,128]{1,0:T(8,128)(2,1)}, bf16[2064,128]{1,0:T(8,128)(2,1)S(1)}, u32[]{:S(2)}, u32[]{:S(2)}) collective-permute-start(bf16[2064,128]{1,0:T(8,128)(2,1)} %prepare_rows.1.refs_0_), channel_id=1, source_target_pairs={{0,4},{1,5},{2,6},{3,7},{4,0},{5,1},{6,2},{7,3},{8,12},{9,13},{10,... | collective-permute-start | bytes 1585160 | tf_op jit(solution)/shard_map/ppermute | solution.py:393
  7.9 1.1 %copy-start = (bf16[2064,128]{1,0:T(8,128)(2,1)S(1)}, bf16[2064,128]{1,0:T(8,128)(2,1)}, u32[]{:S(2)}) copy-start(bf16[2064,128]{1,0:T(8,128)(2,1)} %prepare_rows.1.refs_0_) | copy-start | bytes 1585156
  21.7 9.5 %collective-permute-start.5 = (bf16[2064,128]{1,0:T(8,128)(2,1)S(1)}, bf16[2064,128]{1,0:T(8,128)(2,1)S(1)}, u32[]{:S(2)}, u32[]{:S(2)}) collective-permute-start(bf16[2064,128]{1,0:T(8,128)(2,1)S(1)} %collective-permute-done.1.refs_0_), channel_id=1, source_target_pairs={{0,1},{1,0},{2,3},{3,2},{4,5},{5,4},{6,7},{7,6},{8,9},{9,8},{10,11... | collective-permute-start | bytes 1585160 | tf_op jit(solution)/shard_map/ppermute | solution.py:393
  21.8 9.4 %collective-permute-start.6 = (bf16[2064,128]{1,0:T(8,128)(2,1)S(1)}, bf16[2064,128]{1,0:T(8,128)(2,1)S(1)}, u32[]{:S(2)}, u32[]{:S(2)}) collective-permute-start(bf16[2064,128]{1,0:T(8,128)(2,1)S(1)} %collective-permute-done.2.refs_1_), channel_id=1, source_target_pairs={{0,1},{1,0},{2,3},{3,2},{4,5},{5,4},{6,7},{7,6},{8,9},{9,8},{10,11... | collective-permute-start | bytes 1585160 | tf_op jit(solution)/shard_map/ppermute | solution.py:393
  22.4 8.3 %collective-permute-start.3 = (bf16[1024,128]{1,0:T(8,128)(2,1)S(1)}, bf16[1024,128]{1,0:T(8,128)(2,1)S(1)}, u32[]{:S(2)}, u32[]{:S(2)}) collective-permute-start(bf16[1024,128]{1,0:T(8,128)(2,1)S(1)} %slice.6), channel_id=1, source_target_pairs={{0,4},{1,5},{2,6},{3,7},{4,0},{5,1},{6,2},{7,3},{8,12},{9,13},{10,... | collective-permute-start | bytes 786440 | tf_op jit(solution)/shard_map/ppermute | solution.py:393
  22.9 8.1 %collective-permute-start.4 = (bf16[1040,128]{1,0:T(8,128)(2,1)S(1)}, bf16[1040,128]{1,0:T(8,128)(2,1)S(1)}, u32[]{:S(2)}, u32[]{:S(2)}) collective-permute-start(bf16[1040,128]{1,0:T(8,128)(2,1)S(1)} %slice.7), channel_id=1, source_target_pairs={{0,2},{1,3},{2,0},{3,1},{4,6},{5,7},{6,4},{7,5},{8,10},{9,11},{10,... | collective-permute-start | bytes 798728 | tf_op jit(solution)/shard_map/ppermute | solution.py:393
  29.8 33.0 %copy-start.1 = (s32[8]{0:T(128)S(1)}, s32[8]{0:T(128)}, u32[]{:S(2)}) copy-start(s32[8]{0:T(128)} %slot_ref.1) | copy-start | bytes 100
  31.1 2.0 %collective-permute-start.7 = (bf16[2064,128]{1,0:T(8,128)(2,1)S(1)}, bf16[2064,128]{1,0:T(8,128)(2,1)S(1)}, u32[]{:S(2)}, u32[]{:S(2)}) collective-permute-start(bf16[2064,128]{1,0:T(8,128)(2,1)S(1)} %constant_dynamic-update-slice_fusion.refs_2_), channel_id=1, source_target_pairs={{0,1},{1,0},{2,3},{3,2},{4,5},{5,4},{6,7},{7,6},{8,9},{9,8},{10,11... | collective-permute-start | bytes 1585160 | tf_op jit(solution)/shard_map/ppermute | solution.py:393
  45.0 1.2 %collective-permute-start.8 = (f32[4,1024]{1,0:T(4,128)S(1)}, f32[4,1024]{1,0:T(4,128)S(1)}, u32[]{:S(2)}, u32[]{:S(2)}) collective-permute-start(f32[4,1024]{1,0:T(4,128)S(1)} %constant_dynamic-update-slice_fusion.2.mine_ref), channel_id=1, source_target_pairs={{0,1},{1,0},{2,3},{3,2},{4,5},{5,4},{6,7},{7,6},{8,9},{9,8},{10,11... | collective-permute-start | bytes 49160 | tf_op jit(solution)/shard_map/ppermute | solution.py:393
  46.3 3.8 %collective-permute-start.9 = (f32[4,1024]{1,0:T(4,128)S(1)}, f32[4,1024]{1,0:T(4,128)S(1)}, u32[]{:S(2)}, u32[]{:S(2)}) collective-permute-start(f32[4,1024]{1,0:T(4,128)S(1)} %merge_stats.2.mine_ref), channel_id=1, source_target_pairs={{0,2},{1,3},{2,0},{3,1},{4,6},{5,7},{6,4},{7,5},{8,10},{9,11},{10,... | collective-permute-start | bytes 49160 | tf_op jit(solution)/shard_map/ppermute | solution.py:393
  50.2 3.8 %collective-permute-start.10 = (f32[4,1024]{1,0:T(4,128)S(1)}, f32[4,1024]{1,0:T(4,128)S(1)}, u32[]{:S(2)}, u32[]{:S(2)}) collective-permute-start(f32[4,1024]{1,0:T(4,128)S(1)} %merge_stats.3.refs_0_), channel_id=1, source_target_pairs={{0,4},{1,5},{2,6},{3,7},{4,0},{5,1},{6,2},{7,3},{8,12},{9,13},{10,... | collective-permute-start | bytes 49160 | tf_op jit(solution)/shard_map/ppermute | solution.py:393
  54.0 3.8 %collective-permute-start.11 = (f32[4,1024]{1,0:T(4,128)S(1)}, f32[4,1024]{1,0:T(4,128)S(1)}, u32[]{:S(2)}, u32[]{:S(2)}) collective-permute-start(f32[4,1024]{1,0:T(4,128)S(1)} %finish_rows.1), channel_id=1, source_target_pairs={{0,8},{8,0},{16,24},{24,16},{1,9},{9,1},{17,25},{25,17},{2,10},{10... | collective-permute-start | bytes 49160 | tf_op jit(solution)/shard_map/ppermute | solution.py:438
  57.9 4.9 %collective-permute-start.12 = (f32[8,1024]{1,0:T(8,128)S(1)}, f32[8,1024]{1,0:T(8,128)S(1)}, u32[]{:S(2)}, u32[]{:S(2)}) collective-permute-start(f32[8,1024]{1,0:T(8,128)S(1)} %pad_maximum_fusion.near_ref), channel_id=1, source_target_pairs={{0,16},{8,24},{16,0},{24,8},{1,17},{9,25},{17,1},{25,9},{2,18},{10... | collective-permute-start | bytes 98312 | tf_op jit(solution)/shard_map/ppermute | solution.py:438

commit v3 on v2

--- a/solution.py
+++ b/solution.py
@@ -106,7 +106,7 @@
     def begin():
         if mode == "load":
             for index in range(ahead):
-                arrival(index).start(priority=index % 2)
+                arrival(index).start()
         for place, block in enumerate(blocks):
             rows_ref[:, pl.ds(place * live_cap, live_cap)] = block[...]
         peak_ref[...] = jnp.full(peak_ref.shape, lowest, f32)
@@ -176,7 +176,7 @@
 
                 @pl.when(index + ahead < steps * halves)
                 def _():
-                    arrival(index + ahead).start(priority=(half + ahead) % 2)
+                    arrival(index + ahead).start()
 
             logits_refs[unit % 2][...] = jnp.dot(
                 weight_ref[pl.ds(at, part_vocab), :],
@@ -413,8 +413,9 @@
         diagonal_low, diagonal_high, *second = lax.optimization_barrier((diagonal_low, diagonal_high, *second))
         diagonal = jnp.concatenate((diagonal_low, diagonal_high), axis=0)
         diagonal_other = swap(diagonal, 1, vocab_count)
-        third = block_stats((x_other, y_other, diagonal, diagonal_other), weight_rows, "resident", 400, 2, 512)
-        calls = (first, second, third)
+        third = block_stats((x_other, y_other), weight_rows, "resident", 800, 5)
+        fourth = block_stats((diagonal, diagonal_other), weight_rows, "resident", 800, 5)
+        calls = (first, second, third, fourth)
     else:
         gathered = lax.all_gather(own, "vocab", axis=0)
         calls = [

time: 64.4 us -> 61.7 us (0.958)
  waiting for transfers between devices: 13.1 us -> 11 us
  Pallas kernels: 34.2 us -> 33.3 us
    ppermute x11, waiting for transfers between devices: 8.74 us -> 6.66 us  [swap(): return lax.ppermute(array, 'vocab', [(i, i ^ mask) for i in range(count)])]
    pallas_call x3 -> x4, Pallas kernels: 30 us -> 29 us  [block_stats(): pl.pallas_call(functools.partial(stats_kernel, count, vocab_cols, steps,...]
  transfers between devices with their start and end apart: 13 -> 13, of which waited for: 8 -> 7; matrix products, arithmetic and copies ran while one was open for 0% -> 0% of each run, Pallas kernels for 28% -> 38%
where the time goes in v3:
time: 61.7 us; the launch traced here: 61.5 us
  Pallas kernels  33.3 us (54%)
  starting transfers between devices  15.2 us (25%)
  waiting for transfers between devices  11 us (18%)
  local copies, waits for them, and re-layouts  1.2 us (2%)
  between operations  0.78 us (1%)
    pallas_call x4, Pallas kernels, block_stats(): pl.pallas_call(functools.partial(stats_kernel, count, vocab_cols, steps,...  29 us
    ppermute x11, starting transfers between devices, swap(): return lax.ppermute(array, 'vocab', [(i, i ^ mask) for i in range(count)])  10.9 us
    ppermute x11, waiting for transfers between devices, swap(): return lax.ppermute(array, 'vocab', [(i, i ^ mask) for i in range(count)])  6.66 us
    ppermute x2, waiting for transfers between devices, local(): far = lax.ppermute(near, 'req', [(i, i ^ mask) for i in range(req_count)])  4.39 us
    ppermute x2, starting transfers between devices, local(): far = lax.ppermute(near, 'req', [(i, i ^ mask) for i in range(req_count)])  4.3 us
    pallas_call x1, Pallas kernels, prepare(): pl.pallas_call(prepare_kernel, out_shape=jax.ShapeDtypeStruct((depth + ex...  2.67 us
    pallas_call x1, Pallas kernels, pick(): pl.pallas_call(functools.partial(pick_kernel, vocab_count, paired, seq_le...  1.46 us
  transfers between devices with their start and end apart: 13, of which 7 were waited for; matrix products, arithmetic and copies ran while one was open for 0% of the time, Pallas kernels for 38%

profile of v3, /device:TPU:0, one launch (start us, length us, event | category | flops | bytes accessed | tf_op | source)
XLA Modules:
  0.0 61.5 jit_solution(15224787335105879293)
XLA Ops:
  0.6 2.7 %prepare_rows.1.refs_0_ = bf16[2064,128]{1,0:T(8,128)(2,1)} custom-call(s32[8]{0:T(128)} %lengths_in.1, bf16[192,2048]{1,0:T(8,128)(2,1)} %hidden_in.1, f32[1,2048]{1,0:T(1,128)} %bitcast.4, s32[1,192]{1,0:T(1,128)} %bitcast.5), custom_call_target="tpu_custom_call" | custom-call | tf_op jit(solution)/shard_map/prepare_rows/pallas_call | solution.py:68
  3.3 0.5 collective-permute-start
  3.8 2.6 %collective-permute-start.1 = (bf16[2064,128]{1,0:T(8,128)(2,1)}, bf16[2064,128]{1,0:T(8,128)(2,1)S(1)}, u32[]{:S(2)}, u32[]{:S(2)}) collective-permute-start(bf16[2064,128]{1,0:T(8,128)(2,1)} %prepare_rows.1.refs_0_), channel_id=1, source_target_pairs={{0,2},{1,3},{2,0},{3,1},{4,6},{5,7},{6,4},{7,5},{8,10},{9,11},{10,... | collective-permute-start | bytes 1585160 | tf_op jit(solution)/shard_map/ppermute | solution.py:393
  6.4 1.5 %collective-permute-start.2 = (bf16[2064,128]{1,0:T(8,128)(2,1)}, bf16[2064,128]{1,0:T(8,128)(2,1)S(1)}, u32[]{:S(2)}, u32[]{:S(2)}) collective-permute-start(bf16[2064,128]{1,0:T(8,128)(2,1)} %prepare_rows.1.refs_0_), channel_id=1, source_target_pairs={{0,4},{1,5},{2,6},{3,7},{4,0},{5,1},{6,2},{7,3},{8,12},{9,13},{10,... | collective-permute-start | bytes 1585160 | tf_op jit(solution)/shard_map/ppermute | solution.py:393
  7.9 1.1 %copy-done = bf16[2064,128]{1,0:T(8,128)(2,1)S(1)} copy-done((bf16[2064,128]{1,0:T(8,128)(2,1)S(1)}, bf16[2064,128]{1,0:T(8,128)(2,1)}, u32[]{:S(2)}) %copy-start) | copy-done | bytes 528408
  9.0 12.9 %row_stats.4 = (f32[4,256]{1,0:T(4,128)S(1)}, f32[1,256]{1,0:T(1,128)S(1)}, bf16[4000,2048]{1,0:T(8,128)(2,1)S(1)}) custom-call(bf16[2064,128]{1,0:T(8,128)(2,1)S(1)} %copy-done, bf16[2064,128]{1,0:T(8,128)(2,1)S(1)} %collective-permute-done.refs_1_, bf16[4000,2048]{1,0:T(8,128)(2,1)} %bitcast.3), custom_call_target="tpu_custom_call" | custom-call | flops 4194304000 | bytes 16384000 | tf_op jit(solution)/shard_map/row_stats/pallas_call | solution.py:261
  21.9 0.0 collective-permute-done.1.refs_0_
  21.9 0.1 collective-permute-start.5
  22.0 0.6 collective-permute-start.6
  22.6 0.5 collective-permute-start.3
  23.1 1.5 %collective-permute-start.4 = (bf16[1040,128]{1,0:T(8,128)(2,1)S(1)}, bf16[1040,128]{1,0:T(8,128)(2,1)S(1)}, u32[]{:S(2)}, u32[]{:S(2)}) collective-permute-start(bf16[1040,128]{1,0:T(8,128)(2,1)S(1)} %slice.7), channel_id=1, source_target_pairs={{0,2},{1,3},{2,0},{3,1},{4,6},{5,7},{6,4},{7,5},{8,10},{9,11},{10,... | collective-permute-start | bytes 798728 | tf_op jit(solution)/shard_map/ppermute | solution.py:393
  24.6 5.4 %row_stats.5 = (f32[4,256]{1,0:T(4,128)S(1)}, f32[1,256]{1,0:T(1,128)S(1)}) custom-call(bf16[2064,128]{1,0:T(8,128)(2,1)S(1)} %collective-permute-done.1.refs_0_, bf16[2064,128]{1,0:T(8,128)(2,1)S(1)} %collective-permute-done.2.refs_1_, bf16[4000,2048]{1,0:T(8,128)(2,1)S(1)} %get-tuple-element.22.refs_2_), custom_call_target="tpu_custom_call" | custom-call | flops 4194304000 | bytes 1048576 | tf_op jit(solution)/shard_map/row_stats/pallas_call | solution.py:261
  30.0 0.9 %collective-permute-done.3 = bf16[1024,128]{1,0:T(8,128)(2,1)S(1)} collective-permute-done((bf16[1024,128]{1,0:T(8,128)(2,1)S(1)}, bf16[1024,128]{1,0:T(8,128)(2,1)S(1)}, u32[]{:S(2)}, u32[]{:S(2)}) %collective-permute-start.3) | collective-permute-done | bytes 262176 | tf_op jit(solution)/shard_map/ppermute | solution.py:393
  30.9 0.4 collective-permute-done.4
  31.3 0.1 collective-permute-start.7
  31.4 0.0 copy-start.1
  31.4 0.0 collective-permute-done.5.refs_0_
  31.4 0.0 collective-permute-done.6.refs_1_
  31.4 5.4 %row_stats.6 = (f32[4,256]{1,0:T(4,128)S(1)}, f32[1,256]{1,0:T(1,128)S(1)}) custom-call(bf16[2064,128]{1,0:T(8,128)(2,1)S(1)} %collective-permute-done.5.refs_0_, bf16[2064,128]{1,0:T(8,128)(2,1)S(1)} %collective-permute-done.6.refs_1_, bf16[4000,2048]{1,0:T(8,128)(2,1)S(1)} %get-tuple-element.22.refs_2_), custom_call_target="tpu_custom_call" | custom-call | flops 4194304000 | bytes 1048576 | tf_op jit(solution)/shard_map/row_stats/pallas_call | solution.py:261
  36.9 5.4 %row_stats.7 = (f32[4,256]{1,0:T(4,128)S(1)}, f32[1,256]{1,0:T(1,128)S(1)}) custom-call(bf16[2064,128]{1,0:T(8,128)(2,1)S(1)} %constant_dynamic-update-slice_fusion.refs_0_, bf16[2064,128]{1,0:T(8,128)(2,1)S(1)} %collective-permute-done.7.refs_1_, bf16[4000,2048]{1,0:T(8,128)(2,1)S(1)} %get-tuple-element.22.refs_2_), custom_call_target="tpu_custom_call" | custom-call | flops 4194304000 | bytes 1048576 | tf_op jit(solution)/shard_map/row_stats/pallas_call | solution.py:261
  42.2 0.5 collective-permute-start.8
  42.8 0.8 %collective-permute-done.8.other_ref = f32[4,1024]{1,0:T(4,128)S(1)} collective-permute-done((f32[4,1024]{1,0:T(4,128)S(1)}, f32[4,1024]{1,0:T(4,128)S(1)}, u32[]{:S(2)}, u32[]{:S(2)}) %collective-permute-start.8) | collective-permute-done | bytes 16416 | tf_op jit(solution)/shard_map/ppermute | solution.py:393
  43.7 1.6 %collective-permute-start.9 = (f32[4,1024]{1,0:T(4,128)S(1)}, f32[4,1024]{1,0:T(4,128)S(1)}, u32[]{:S(2)}, u32[]{:S(2)}) collective-permute-start(f32[4,1024]{1,0:T(4,128)S(1)} %merge_stats.2.mine_ref), channel_id=1, source_target_pairs={{0,2},{1,3},{2,0},{3,1},{4,6},{5,7},{6,4},{7,5},{8,10},{9,11},{10,... | collective-permute-start | bytes 49160 | tf_op jit(solution)/shard_map/ppermute | solution.py:393
  45.2 2.2 %collective-permute-done.9.other_ref = f32[4,1024]{1,0:T(4,128)S(1)} collective-permute-done((f32[4,1024]{1,0:T(4,128)S(1)}, f32[4,1024]{1,0:T(4,128)S(1)}, u32[]{:S(2)}, u32[]{:S(2)}) %collective-permute-start.9) | collective-permute-done | bytes 16416 | tf_op jit(solution)/shard_map/ppermute | solution.py:393
  47.5 1.5 %collective-permute-start.10 = (f32[4,1024]{1,0:T(4,128)S(1)}, f32[4,1024]{1,0:T(4,128)S(1)}, u32[]{:S(2)}, u32[]{:S(2)}) collective-permute-start(f32[4,1024]{1,0:T(4,128)S(1)} %merge_stats.3.refs_0_), channel_id=1, source_target_pairs={{0,4},{1,5},{2,6},{3,7},{4,0},{5,1},{6,2},{7,3},{8,12},{9,13},{10,... | collective-permute-start | bytes 49160 | tf_op jit(solution)/shard_map/ppermute | solution.py:393
  49.0 2.3 %collective-permute-done.10.refs_1_ = f32[4,1024]{1,0:T(4,128)S(1)} collective-permute-done((f32[4,1024]{1,0:T(4,128)S(1)}, f32[4,1024]{1,0:T(4,128)S(1)}, u32[]{:S(2)}, u32[]{:S(2)}) %collective-permute-start.10) | collective-permute-done | bytes 16416 | tf_op jit(solution)/shard_map/ppermute | solution.py:393
  51.3 0.1 finish_rows.1
  51.4 1.6 %collective-permute-start.11 = (f32[4,1024]{1,0:T(4,128)S(1)}, f32[4,1024]{1,0:T(4,128)S(1)}, u32[]{:S(2)}, u32[]{:S(2)}) collective-permute-start(f32[4,1024]{1,0:T(4,128)S(1)} %finish_rows.1), channel_id=1, source_target_pairs={{0,8},{8,0},{16,24},{24,16},{1,9},{9,1},{17,25},{25,17},{2,10},{10... | collective-permute-start | bytes 49160 | tf_op jit(solution)/shard_map/ppermute | solution.py:439
  53.0 2.2 %collective-permute-done.11 = f32[4,1024]{1,0:T(4,128)S(1)} collective-permute-done((f32[4,1024]{1,0:T(4,128)S(1)}, f32[4,1024]{1,0:T(4,128)S(1)}, u32[]{:S(2)}, u32[]{:S(2)}) %collective-permute-start.11) | collective-permute-done | bytes 16416 | tf_op jit(solution)/shard_map/ppermute | solution.py:439
  55.2 2.7 %collective-permute-start.12 = (f32[8,1024]{1,0:T(8,128)S(1)}, f32[8,1024]{1,0:T(8,128)S(1)}, u32[]{:S(2)}, u32[]{:S(2)}) collective-permute-start(f32[8,1024]{1,0:T(8,128)S(1)} %pad_maximum_fusion.near_ref), channel_id=1, source_target_pairs={{0,16},{8,24},{16,0},{24,8},{1,17},{9,25},{17,1},{25,9},{2,18},{10... | collective-permute-start | bytes 98312 | tf_op jit(solution)/shard_map/ppermute | solution.py:439
  57.8 2.2 %collective-permute-done.12.far_ref = f32[8,1024]{1,0:T(8,128)S(1)} collective-permute-done((f32[8,1024]{1,0:T(8,128)S(1)}, f32[8,1024]{1,0:T(8,128)S(1)}, u32[]{:S(2)}, u32[]{:S(2)}) %collective-permute-start.12) | collective-permute-done | bytes 32800 | tf_op jit(solution)/shard_map/ppermute | solution.py:439
  60.1 1.5 %pick_requests.1 = (f32[8,24]{1,0:T(8,128)}, f32[8,24]{1,0:T(8,128)}) custom-call(s32[8]{0:T(128)S(1)} %copy-done.1, f32[8,1024]{1,0:T(8,128)S(1)} %pad_maximum_fusion.near_ref, f32[8,1024]{1,0:T(8,128)S(1)} %collective-permute-done.12.far_ref), custom_call_target="tpu_custom_call" | custom-call | tf_op jit(solution)/shard_map/pick_requests/pallas_call | solution.py:376
  (17 shorter events, 0.2 us)
Async XLA Ops:
  3.3 4.6 %collective-permute-start = (bf16[2064,128]{1,0:T(8,128)(2,1)}, bf16[2064,128]{1,0:T(8,128)(2,1)S(1)}, u32[]{:S(2)}, u32[]{:S(2)}) collective-permute-start(bf16[2064,128]{1,0:T(8,128)(2,1)} %prepare_rows.1.refs_0_), channel_id=1, source_target_pairs={{0,1},{1,0},{2,3},{3,2},{4,5},{5,4},{6,7},{7,6},{8,9},{9,8},{10,11... | collective-permute-start | bytes 1585160 | tf_op jit(solution)/shard_map/ppermute | solution.py:393
  3.8 18.0 %collective-permute-start.1 = (bf16[2064,128]{1,0:T(8,128)(2,1)}, bf16[2064,128]{1,0:T(8,128)(2,1)S(1)}, u32[]{:S(2)}, u32[]{:S(2)}) collective-permute-start(bf16[2064,128]{1,0:T(8,128)(2,1)} %prepare_rows.1.refs_0_), channel_id=1, source_target_pairs={{0,2},{1,3},{2,0},{3,1},{4,6},{5,7},{6,4},{7,5},{8,10},{9,11},{10,... | collective-permute-start | bytes 1585160 | tf_op jit(solution)/shard_map/ppermute | solution.py:393
  6.4 15.5 %collective-permute-start.2 = (bf16[2064,128]{1,0:T(8,128)(2,1)}, bf16[2064,128]{1,0:T(8,128)(2,1)S(1)}, u32[]{:S(2)}, u32[]{:S(2)}) collective-permute-start(bf16[2064,128]{1,0:T(8,128)(2,1)} %prepare_rows.1.refs_0_), channel_id=1, source_target_pairs={{0,4},{1,5},{2,6},{3,7},{4,0},{5,1},{6,2},{7,3},{8,12},{9,13},{10,... | collective-permute-start | bytes 1585160 | tf_op jit(solution)/shard_map/ppermute | solution.py:393
  7.9 1.1 %copy-start = (bf16[2064,128]{1,0:T(8,128)(2,1)S(1)}, bf16[2064,128]{1,0:T(8,128)(2,1)}, u32[]{:S(2)}) copy-start(bf16[2064,128]{1,0:T(8,128)(2,1)} %prepare_rows.1.refs_0_) | copy-start | bytes 1585156
  21.9 9.5 %collective-permute-start.5 = (bf16[2064,128]{1,0:T(8,128)(2,1)S(1)}, bf16[2064,128]{1,0:T(8,128)(2,1)S(1)}, u32[]{:S(2)}, u32[]{:S(2)}) collective-permute-start(bf16[2064,128]{1,0:T(8,128)(2,1)S(1)} %collective-permute-done.1.refs_0_), channel_id=1, source_target_pairs={{0,1},{1,0},{2,3},{3,2},{4,5},{5,4},{6,7},{7,6},{8,9},{9,8},{10,11... | collective-permute-start | bytes 1585160 | tf_op jit(solution)/shard_map/ppermute | solution.py:393
  22.0 9.4 %collective-permute-start.6 = (bf16[2064,128]{1,0:T(8,128)(2,1)S(1)}, bf16[2064,128]{1,0:T(8,128)(2,1)S(1)}, u32[]{:S(2)}, u32[]{:S(2)}) collective-permute-start(bf16[2064,128]{1,0:T(8,128)(2,1)S(1)} %collective-permute-done.2.refs_1_), channel_id=1, source_target_pairs={{0,1},{1,0},{2,3},{3,2},{4,5},{5,4},{6,7},{7,6},{8,9},{9,8},{10,11... | collective-permute-start | bytes 1585160 | tf_op jit(solution)/shard_map/ppermute | solution.py:393
  22.6 8.3 %collective-permute-start.3 = (bf16[1024,128]{1,0:T(8,128)(2,1)S(1)}, bf16[1024,128]{1,0:T(8,128)(2,1)S(1)}, u32[]{:S(2)}, u32[]{:S(2)}) collective-permute-start(bf16[1024,128]{1,0:T(8,128)(2,1)S(1)} %slice.6), channel_id=1, source_target_pairs={{0,4},{1,5},{2,6},{3,7},{4,0},{5,1},{6,2},{7,3},{8,12},{9,13},{10,... | collective-permute-start | bytes 786440 | tf_op jit(solution)/shard_map/ppermute | solution.py:393
  23.1 8.1 %collective-permute-start.4 = (bf16[1040,128]{1,0:T(8,128)(2,1)S(1)}, bf16[1040,128]{1,0:T(8,128)(2,1)S(1)}, u32[]{:S(2)}, u32[]{:S(2)}) collective-permute-start(bf16[1040,128]{1,0:T(8,128)(2,1)S(1)} %slice.7), channel_id=1, source_target_pairs={{0,2},{1,3},{2,0},{3,1},{4,6},{5,7},{6,4},{7,5},{8,10},{9,11},{10,... | collective-permute-start | bytes 798728 | tf_op jit(solution)/shard_map/ppermute | solution.py:393
  31.3 5.5 %collective-permute-start.7 = (bf16[2064,128]{1,0:T(8,128)(2,1)S(1)}, bf16[2064,128]{1,0:T(8,128)(2,1)S(1)}, u32[]{:S(2)}, u32[]{:S(2)}) collective-permute-start(bf16[2064,128]{1,0:T(8,128)(2,1)S(1)} %constant_dynamic-update-slice_fusion.refs_0_), channel_id=1, source_target_pairs={{0,1},{1,0},{2,3},{3,2},{4,5},{5,4},{6,7},{7,6},{8,9},{9,8},{10,11... | collective-permute-start | bytes 1585160 | tf_op jit(solution)/shard_map/ppermute | solution.py:393
  31.4 28.6 %copy-start.1 = (s32[8]{0:T(128)S(1)}, s32[8]{0:T(128)}, u32[]{:S(2)}) copy-start(s32[8]{0:T(128)} %slot_ref.1) | copy-start | bytes 100
  42.2 1.4 %collective-permute-start.8 = (f32[4,1024]{1,0:T(4,128)S(1)}, f32[4,1024]{1,0:T(4,128)S(1)}, u32[]{:S(2)}, u32[]{:S(2)}) collective-permute-start(f32[4,1024]{1,0:T(4,128)S(1)} %constant_dynamic-update-slice_fusion.2.mine_ref), channel_id=1, source_target_pairs={{0,1},{1,0},{2,3},{3,2},{4,5},{5,4},{6,7},{7,6},{8,9},{9,8},{10,11... | collective-permute-start | bytes 49160 | tf_op jit(solution)/shard_map/ppermute | solution.py:393
  43.7 3.8 %collective-permute-start.9 = (f32[4,1024]{1,0:T(4,128)S(1)}, f32[4,1024]{1,0:T(4,128)S(1)}, u32[]{:S(2)}, u32[]{:S(2)}) collective-permute-start(f32[4,1024]{1,0:T(4,128)S(1)} %merge_stats.2.mine_ref), channel_id=1, source_target_pairs={{0,2},{1,3},{2,0},{3,1},{4,6},{5,7},{6,4},{7,5},{8,10},{9,11},{10,... | collective-permute-start | bytes 49160 | tf_op jit(solution)/shard_map/ppermute | solution.py:393
  47.5 3.8 %collective-permute-start.10 = (f32[4,1024]{1,0:T(4,128)S(1)}, f32[4,1024]{1,0:T(4,128)S(1)}, u32[]{:S(2)}, u32[]{:S(2)}) collective-permute-start(f32[4,1024]{1,0:T(4,128)S(1)} %merge_stats.3.refs_0_), channel_id=1, source_target_pairs={{0,4},{1,5},{2,6},{3,7},{4,0},{5,1},{6,2},{7,3},{8,12},{9,13},{10,... | collective-permute-start | bytes 49160 | tf_op jit(solution)/shard_map/ppermute | solution.py:393
  51.4 3.8 %collective-permute-start.11 = (f32[4,1024]{1,0:T(4,128)S(1)}, f32[4,1024]{1,0:T(4,128)S(1)}, u32[]{:S(2)}, u32[]{:S(2)}) collective-permute-start(f32[4,1024]{1,0:T(4,128)S(1)} %finish_rows.1), channel_id=1, source_target_pairs={{0,8},{8,0},{16,24},{24,16},{1,9},{9,1},{17,25},{25,17},{2,10},{10... | collective-permute-start | bytes 49160 | tf_op jit(solution)/shard_map/ppermute | solution.py:439
  55.2 4.9 %collective-permute-start.12 = (f32[8,1024]{1,0:T(8,128)S(1)}, f32[8,1024]{1,0:T(8,128)S(1)}, u32[]{:S(2)}, u32[]{:S(2)}) collective-permute-start(f32[8,1024]{1,0:T(8,128)S(1)} %pad_maximum_fusion.near_ref), channel_id=1, source_target_pairs={{0,16},{8,24},{16,0},{24,8},{1,17},{9,25},{17,1},{25,9},{2,18},{10... | collective-permute-start | bytes 98312 | tf_op jit(solution)/shard_map/ppermute | solution.py:439

commit v4 on v3

--- a/solution.py
+++ b/solution.py
@@ -402,7 +402,7 @@
         x_same = swap(own, 2, vocab_count)
         y_same = swap(own, 4, vocab_count)
         core = swap(own, 1, vocab_count)
-        *first, weight_rows = block_stats((own, core), weight_rows, "load")
+        *first, weight_rows = block_stats((own, core), weight_rows, "load", 800, 5)
         x_same, y_same, weight_rows = lax.optimization_barrier((x_same, y_same, weight_rows))
         half = own.shape[0] // 32 * 16
         diagonal_low = swap(x_same[:half], 4, vocab_count)

time: 61.7 us -> 61.6 us (level)
  waiting for transfers between devices: 11 us -> 14.6 us
  starting transfers between devices: 15.2 us -> 13.4 us
  Pallas kernels: 33.3 us -> 31.5 us
    ppermute x11, waiting for transfers between devices: 6.66 us -> 10.2 us  [swap(): return lax.ppermute(array, 'vocab', [(i, i ^ mask) for i in range(count)])]
    ppermute x11, starting transfers between devices: 10.9 us -> 9.07 us  [swap(): return lax.ppermute(array, 'vocab', [(i, i ^ mask) for i in range(count)])]
    pallas_call x4, Pallas kernels: 29 us -> 27.3 us  [block_stats(): pl.pallas_call(functools.partial(stats_kernel, count, vocab_cols, steps,...]
  transfers between devices with their start and end apart: 13 -> 13, of which waited for: 7 -> 8; matrix products, arithmetic and copies ran while one was open for 0% -> 0% of each run, Pallas kernels for 38% -> 36%
where the time goes in v4:
time: 61.6 us; the launch traced here: 61.4 us
  Pallas kernels  31.5 us (51%)
  waiting for transfers between devices  14.6 us (24%)
  starting transfers between devices  13.4 us (22%)
  local copies, waits for them, and re-layouts  1.2 us (2%)
  between operations  0.77 us (1%)
    pallas_call x4, Pallas kernels, block_stats(): pl.pallas_call(functools.partial(stats_kernel, count, vocab_cols, steps,...  27.3 us
    ppermute x11, waiting for transfers between devices, swap(): return lax.ppermute(array, 'vocab', [(i, i ^ mask) for i in range(count)])  10.2 us
    ppermute x11, starting transfers between devices, swap(): return lax.ppermute(array, 'vocab', [(i, i ^ mask) for i in range(count)])  9.07 us
    ppermute x2, waiting for transfers between devices, local(): far = lax.ppermute(near, 'req', [(i, i ^ mask) for i in range(req_count)])  4.39 us
    ppermute x2, starting transfers between devices, local(): far = lax.ppermute(near, 'req', [(i, i ^ mask) for i in range(req_count)])  4.29 us
    pallas_call x1, Pallas kernels, prepare(): pl.pallas_call(prepare_kernel, out_shape=jax.ShapeDtypeStruct((depth + ex...  2.67 us
    pallas_call x1, Pallas kernels, pick(): pl.pallas_call(functools.partial(pick_kernel, vocab_count, paired, seq_le...  1.46 us
  transfers between devices with their start and end apart: 13, of which 8 were waited for; matrix products, arithmetic and copies ran while one was open for 0% of the time, Pallas kernels for 36%

profile of v4, /device:TPU:0, one launch (start us, length us, event | category | flops | bytes accessed | tf_op | source)
XLA Modules:
  0.0 61.4 jit_solution(3789472441412612932)
XLA Ops:
  0.6 2.7 %prepare_rows.1.refs_0_ = bf16[2064,128]{1,0:T(8,128)(2,1)} custom-call(s32[8]{0:T(128)} %lengths_in.1, bf16[192,2048]{1,0:T(8,128)(2,1)} %hidden_in.1, f32[1,2048]{1,0:T(1,128)} %bitcast.4, s32[1,192]{1,0:T(1,128)} %bitcast.5), custom_call_target="tpu_custom_call" | custom-call | tf_op jit(solution)/shard_map/prepare_rows/pallas_call | solution.py:68
  3.3 0.5 collective-permute-start
  3.8 2.6 %collective-permute-start.1 = (bf16[2064,128]{1,0:T(8,128)(2,1)}, bf16[2064,128]{1,0:T(8,128)(2,1)S(1)}, u32[]{:S(2)}, u32[]{:S(2)}) collective-permute-start(bf16[2064,128]{1,0:T(8,128)(2,1)} %prepare_rows.1.refs_0_), channel_id=1, source_target_pairs={{0,2},{1,3},{2,0},{3,1},{4,6},{5,7},{6,4},{7,5},{8,10},{9,11},{10,... | collective-permute-start | bytes 1585160 | tf_op jit(solution)/shard_map/ppermute | solution.py:393
  6.4 1.5 %collective-permute-start.2 = (bf16[2064,128]{1,0:T(8,128)(2,1)}, bf16[2064,128]{1,0:T(8,128)(2,1)S(1)}, u32[]{:S(2)}, u32[]{:S(2)}) collective-permute-start(bf16[2064,128]{1,0:T(8,128)(2,1)} %prepare_rows.1.refs_0_), channel_id=1, source_target_pairs={{0,4},{1,5},{2,6},{3,7},{4,0},{5,1},{6,2},{7,3},{8,12},{9,13},{10,... | collective-permute-start | bytes 1585160 | tf_op jit(solution)/shard_map/ppermute | solution.py:393
  7.9 1.1 %copy-done = bf16[2064,128]{1,0:T(8,128)(2,1)S(1)} copy-done((bf16[2064,128]{1,0:T(8,128)(2,1)S(1)}, bf16[2064,128]{1,0:T(8,128)(2,1)}, u32[]{:S(2)}) %copy-start) | copy-done | bytes 528408
  9.0 11.0 %row_stats.4 = (f32[4,256]{1,0:T(4,128)S(1)}, f32[1,256]{1,0:T(1,128)S(1)}, bf16[4000,2048]{1,0:T(8,128)(2,1)S(1)}) custom-call(bf16[2064,128]{1,0:T(8,128)(2,1)S(1)} %copy-done, bf16[2064,128]{1,0:T(8,128)(2,1)S(1)} %collective-permute-done.refs_1_, bf16[4000,2048]{1,0:T(8,128)(2,1)} %bitcast.3), custom_call_target="tpu_custom_call" | custom-call | flops 4194304000 | bytes 16384000 | tf_op jit(solution)/shard_map/row_stats/pallas_call | solution.py:261
  20.0 0.7 %collective-permute-done.2.refs_1_ = bf16[2064,128]{1,0:T(8,128)(2,1)S(1)} collective-permute-done((bf16[2064,128]{1,0:T(8,128)(2,1)}, bf16[2064,128]{1,0:T(8,128)(2,1)S(1)}, u32[]{:S(2)}, u32[]{:S(2)}) %collective-permute-start.2) | collective-permute-done | bytes 528416 | tf_op jit(solution)/shard_map/ppermute | solution.py:393
  20.7 0.1 collective-permute-start.5
  20.8 0.6 collective-permute-start.6
  21.4 1.5 %collective-permute-start.3 = (bf16[1024,128]{1,0:T(8,128)(2,1)S(1)}, bf16[1024,128]{1,0:T(8,128)(2,1)S(1)}, u32[]{:S(2)}, u32[]{:S(2)}) collective-permute-start(bf16[1024,128]{1,0:T(8,128)(2,1)S(1)} %slice.6), channel_id=1, source_target_pairs={{0,4},{1,5},{2,6},{3,7},{4,0},{5,1},{6,2},{7,3},{8,12},{9,13},{10,... | collective-permute-start | bytes 786440 | tf_op jit(solution)/shard_map/ppermute | solution.py:393
  22.9 0.5 collective-permute-start.4
  23.4 5.4 %row_stats.5 = (f32[4,256]{1,0:T(4,128)S(1)}, f32[1,256]{1,0:T(1,128)S(1)}) custom-call(bf16[2064,128]{1,0:T(8,128)(2,1)S(1)} %collective-permute-done.1.refs_0_, bf16[2064,128]{1,0:T(8,128)(2,1)S(1)} %collective-permute-done.2.refs_1_, bf16[4000,2048]{1,0:T(8,128)(2,1)S(1)} %get-tuple-element.22.refs_2_), custom_call_target="tpu_custom_call" | custom-call | flops 4194304000 | bytes 1048576 | tf_op jit(solution)/shard_map/row_stats/pallas_call | solution.py:261
  28.8 0.8 %collective-permute-done.3 = bf16[1024,128]{1,0:T(8,128)(2,1)S(1)} collective-permute-done((bf16[1024,128]{1,0:T(8,128)(2,1)S(1)}, bf16[1024,128]{1,0:T(8,128)(2,1)S(1)}, u32[]{:S(2)}, u32[]{:S(2)}) %collective-permute-start.3) | collective-permute-done | bytes 262176 | tf_op jit(solution)/shard_map/ppermute | solution.py:393
  29.7 1.3 %collective-permute-done.4 = bf16[1040,128]{1,0:T(8,128)(2,1)S(1)} collective-permute-done((bf16[1040,128]{1,0:T(8,128)(2,1)S(1)}, bf16[1040,128]{1,0:T(8,128)(2,1)S(1)}, u32[]{:S(2)}, u32[]{:S(2)}) %collective-permute-start.4) | collective-permute-done | bytes 266272 | tf_op jit(solution)/shard_map/ppermute | solution.py:393
  31.1 0.1 collective-permute-start.7
  31.2 0.0 copy-start.1
  31.2 0.0 collective-permute-done.5.refs_0_
  31.2 5.6 %row_stats.6 = (f32[4,256]{1,0:T(4,128)S(1)}, f32[1,256]{1,0:T(1,128)S(1)}) custom-call(bf16[2064,128]{1,0:T(8,128)(2,1)S(1)} %collective-permute-done.5.refs_0_, bf16[2064,128]{1,0:T(8,128)(2,1)S(1)} %collective-permute-done.6.refs_1_, bf16[4000,2048]{1,0:T(8,128)(2,1)S(1)} %get-tuple-element.22.refs_2_), custom_call_target="tpu_custom_call" | custom-call | flops 4194304000 | bytes 1048576 | tf_op jit(solution)/shard_map/row_stats/pallas_call | solution.py:261
  36.8 0.0 collective-permute-done.7.refs_1_
  36.8 5.4 %row_stats.7 = (f32[4,256]{1,0:T(4,128)S(1)}, f32[1,256]{1,0:T(1,128)S(1)}) custom-call(bf16[2064,128]{1,0:T(8,128)(2,1)S(1)} %constant_dynamic-update-slice_fusion.refs_0_, bf16[2064,128]{1,0:T(8,128)(2,1)S(1)} %collective-permute-done.7.refs_1_, bf16[4000,2048]{1,0:T(8,128)(2,1)S(1)} %get-tuple-element.22.refs_2_), custom_call_target="tpu_custom_call" | custom-call | flops 4194304000 | bytes 1048576 | tf_op jit(solution)/shard_map/row_stats/pallas_call | solution.py:261
  42.2 0.5 collective-permute-start.8
  42.7 0.8 %collective-permute-done.8.other_ref = f32[4,1024]{1,0:T(4,128)S(1)} collective-permute-done((f32[4,1024]{1,0:T(4,128)S(1)}, f32[4,1024]{1,0:T(4,128)S(1)}, u32[]{:S(2)}, u32[]{:S(2)}) %collective-permute-start.8) | collective-permute-done | bytes 16416 | tf_op jit(solution)/shard_map/ppermute | solution.py:393
  43.6 0.6 collective-permute-start.9
  44.2 3.2 %collective-permute-done.9.other_ref = f32[4,1024]{1,0:T(4,128)S(1)} collective-permute-done((f32[4,1024]{1,0:T(4,128)S(1)}, f32[4,1024]{1,0:T(4,128)S(1)}, u32[]{:S(2)}, u32[]{:S(2)}) %collective-permute-start.9) | collective-permute-done | bytes 16416 | tf_op jit(solution)/shard_map/ppermute | solution.py:393
  47.4 0.6 collective-permute-start.10
  48.0 3.2 %collective-permute-done.10.refs_1_ = f32[4,1024]{1,0:T(4,128)S(1)} collective-permute-done((f32[4,1024]{1,0:T(4,128)S(1)}, f32[4,1024]{1,0:T(4,128)S(1)}, u32[]{:S(2)}, u32[]{:S(2)}) %collective-permute-start.10) | collective-permute-done | bytes 16416 | tf_op jit(solution)/shard_map/ppermute | solution.py:393
  51.2 0.1 finish_rows.1
  51.3 1.6 %collective-permute-start.11 = (f32[4,1024]{1,0:T(4,128)S(1)}, f32[4,1024]{1,0:T(4,128)S(1)}, u32[]{:S(2)}, u32[]{:S(2)}) collective-permute-start(f32[4,1024]{1,0:T(4,128)S(1)} %finish_rows.1), channel_id=1, source_target_pairs={{0,8},{8,0},{16,24},{24,16},{1,9},{9,1},{17,25},{25,17},{2,10},{10... | collective-permute-start | bytes 49160 | tf_op jit(solution)/shard_map/ppermute | solution.py:439
  52.9 2.2 %collective-permute-done.11 = f32[4,1024]{1,0:T(4,128)S(1)} collective-permute-done((f32[4,1024]{1,0:T(4,128)S(1)}, f32[4,1024]{1,0:T(4,128)S(1)}, u32[]{:S(2)}, u32[]{:S(2)}) %collective-permute-start.11) | collective-permute-done | bytes 16416 | tf_op jit(solution)/shard_map/ppermute | solution.py:439
  55.1 2.7 %collective-permute-start.12 = (f32[8,1024]{1,0:T(8,128)S(1)}, f32[8,1024]{1,0:T(8,128)S(1)}, u32[]{:S(2)}, u32[]{:S(2)}) collective-permute-start(f32[8,1024]{1,0:T(8,128)S(1)} %pad_maximum_fusion.near_ref), channel_id=1, source_target_pairs={{0,16},{8,24},{16,0},{24,8},{1,17},{9,25},{17,1},{25,9},{2,18},{10... | collective-permute-start | bytes 98312 | tf_op jit(solution)/shard_map/ppermute | solution.py:439
  57.8 2.2 %collective-permute-done.12.far_ref = f32[8,1024]{1,0:T(8,128)S(1)} collective-permute-done((f32[8,1024]{1,0:T(8,128)S(1)}, f32[8,1024]{1,0:T(8,128)S(1)}, u32[]{:S(2)}, u32[]{:S(2)}) %collective-permute-start.12) | collective-permute-done | bytes 32800 | tf_op jit(solution)/shard_map/ppermute | solution.py:439
  60.0 1.5 %pick_requests.1 = (f32[8,24]{1,0:T(8,128)}, f32[8,24]{1,0:T(8,128)}) custom-call(s32[8]{0:T(128)S(1)} %copy-done.1, f32[8,1024]{1,0:T(8,128)S(1)} %pad_maximum_fusion.near_ref, f32[8,1024]{1,0:T(8,128)S(1)} %collective-permute-done.12.far_ref), custom_call_target="tpu_custom_call" | custom-call | tf_op jit(solution)/shard_map/pick_requests/pallas_call | solution.py:376
  (17 shorter events, 0.2 us)
Async XLA Ops:
  3.3 4.6 %collective-permute-start = (bf16[2064,128]{1,0:T(8,128)(2,1)}, bf16[2064,128]{1,0:T(8,128)(2,1)S(1)}, u32[]{:S(2)}, u32[]{:S(2)}) collective-permute-start(bf16[2064,128]{1,0:T(8,128)(2,1)} %prepare_rows.1.refs_0_), channel_id=1, source_target_pairs={{0,1},{1,0},{2,3},{3,2},{4,5},{5,4},{6,7},{7,6},{8,9},{9,8},{10,11... | collective-permute-start | bytes 1585160 | tf_op jit(solution)/shard_map/ppermute | solution.py:393
  3.8 16.1 %collective-permute-start.1 = (bf16[2064,128]{1,0:T(8,128)(2,1)}, bf16[2064,128]{1,0:T(8,128)(2,1)S(1)}, u32[]{:S(2)}, u32[]{:S(2)}) collective-permute-start(bf16[2064,128]{1,0:T(8,128)(2,1)} %prepare_rows.1.refs_0_), channel_id=1, source_target_pairs={{0,2},{1,3},{2,0},{3,1},{4,6},{5,7},{6,4},{7,5},{8,10},{9,11},{10,... | collective-permute-start | bytes 1585160 | tf_op jit(solution)/shard_map/ppermute | solution.py:393
  6.4 14.3 %collective-permute-start.2 = (bf16[2064,128]{1,0:T(8,128)(2,1)}, bf16[2064,128]{1,0:T(8,128)(2,1)S(1)}, u32[]{:S(2)}, u32[]{:S(2)}) collective-permute-start(bf16[2064,128]{1,0:T(8,128)(2,1)} %prepare_rows.1.refs_0_), channel_id=1, source_target_pairs={{0,4},{1,5},{2,6},{3,7},{4,0},{5,1},{6,2},{7,3},{8,12},{9,13},{10,... | collective-permute-start | bytes 1585160 | tf_op jit(solution)/shard_map/ppermute | solution.py:393
  7.9 1.1 %copy-start = (bf16[2064,128]{1,0:T(8,128)(2,1)S(1)}, bf16[2064,128]{1,0:T(8,128)(2,1)}, u32[]{:S(2)}) copy-start(bf16[2064,128]{1,0:T(8,128)(2,1)} %prepare_rows.1.refs_0_) | copy-start | bytes 1585156
  20.7 10.5 %collective-permute-start.5 = (bf16[2064,128]{1,0:T(8,128)(2,1)S(1)}, bf16[2064,128]{1,0:T(8,128)(2,1)S(1)}, u32[]{:S(2)}, u32[]{:S(2)}) collective-permute-start(bf16[2064,128]{1,0:T(8,128)(2,1)S(1)} %collective-permute-done.1.refs_0_), channel_id=1, source_target_pairs={{0,1},{1,0},{2,3},{3,2},{4,5},{5,4},{6,7},{7,6},{8,9},{9,8},{10,11... | collective-permute-start | bytes 1585160 | tf_op jit(solution)/shard_map/ppermute | solution.py:393
  20.8 10.4 %collective-permute-start.6 = (bf16[2064,128]{1,0:T(8,128)(2,1)S(1)}, bf16[2064,128]{1,0:T(8,128)(2,1)S(1)}, u32[]{:S(2)}, u32[]{:S(2)}) collective-permute-start(bf16[2064,128]{1,0:T(8,128)(2,1)S(1)} %collective-permute-done.2.refs_1_), channel_id=1, source_target_pairs={{0,1},{1,0},{2,3},{3,2},{4,5},{5,4},{6,7},{7,6},{8,9},{9,8},{10,11... | collective-permute-start | bytes 1585160 | tf_op jit(solution)/shard_map/ppermute | solution.py:393
  21.4 8.3 %collective-permute-start.3 = (bf16[1024,128]{1,0:T(8,128)(2,1)S(1)}, bf16[1024,128]{1,0:T(8,128)(2,1)S(1)}, u32[]{:S(2)}, u32[]{:S(2)}) collective-permute-start(bf16[1024,128]{1,0:T(8,128)(2,1)S(1)} %slice.6), channel_id=1, source_target_pairs={{0,4},{1,5},{2,6},{3,7},{4,0},{5,1},{6,2},{7,3},{8,12},{9,13},{10,... | collective-permute-start | bytes 786440 | tf_op jit(solution)/shard_map/ppermute | solution.py:393
  22.9 8.1 %collective-permute-start.4 = (bf16[1040,128]{1,0:T(8,128)(2,1)S(1)}, bf16[1040,128]{1,0:T(8,128)(2,1)S(1)}, u32[]{:S(2)}, u32[]{:S(2)}) collective-permute-start(bf16[1040,128]{1,0:T(8,128)(2,1)S(1)} %slice.7), channel_id=1, source_target_pairs={{0,2},{1,3},{2,0},{3,1},{4,6},{5,7},{6,4},{7,5},{8,10},{9,11},{10,... | collective-permute-start | bytes 798728 | tf_op jit(solution)/shard_map/ppermute | solution.py:393
  31.1 5.7 %collective-permute-start.7 = (bf16[2064,128]{1,0:T(8,128)(2,1)S(1)}, bf16[2064,128]{1,0:T(8,128)(2,1)S(1)}, u32[]{:S(2)}, u32[]{:S(2)}) collective-permute-start(bf16[2064,128]{1,0:T(8,128)(2,1)S(1)} %constant_dynamic-update-slice_fusion.refs_0_), channel_id=1, source_target_pairs={{0,1},{1,0},{2,3},{3,2},{4,5},{5,4},{6,7},{7,6},{8,9},{9,8},{10,11... | collective-permute-start | bytes 1585160 | tf_op jit(solution)/shard_map/ppermute | solution.py:393
  31.2 28.8 %copy-start.1 = (s32[8]{0:T(128)S(1)}, s32[8]{0:T(128)}, u32[]{:S(2)}) copy-start(s32[8]{0:T(128)} %slot_ref.1) | copy-start | bytes 100
  42.2 1.4 %collective-permute-start.8 = (f32[4,1024]{1,0:T(4,128)S(1)}, f32[4,1024]{1,0:T(4,128)S(1)}, u32[]{:S(2)}, u32[]{:S(2)}) collective-permute-start(f32[4,1024]{1,0:T(4,128)S(1)} %constant_dynamic-update-slice_fusion.2.mine_ref), channel_id=1, source_target_pairs={{0,1},{1,0},{2,3},{3,2},{4,5},{5,4},{6,7},{7,6},{8,9},{9,8},{10,11... | collective-permute-start | bytes 49160 | tf_op jit(solution)/shard_map/ppermute | solution.py:393
  43.6 3.8 %collective-permute-start.9 = (f32[4,1024]{1,0:T(4,128)S(1)}, f32[4,1024]{1,0:T(4,128)S(1)}, u32[]{:S(2)}, u32[]{:S(2)}) collective-permute-start(f32[4,1024]{1,0:T(4,128)S(1)} %merge_stats.2.mine_ref), channel_id=1, source_target_pairs={{0,2},{1,3},{2,0},{3,1},{4,6},{5,7},{6,4},{7,5},{8,10},{9,11},{10,... | collective-permute-start | bytes 49160 | tf_op jit(solution)/shard_map/ppermute | solution.py:393
  47.4 3.8 %collective-permute-start.10 = (f32[4,1024]{1,0:T(4,128)S(1)}, f32[4,1024]{1,0:T(4,128)S(1)}, u32[]{:S(2)}, u32[]{:S(2)}) collective-permute-start(f32[4,1024]{1,0:T(4,128)S(1)} %merge_stats.3.refs_0_), channel_id=1, source_target_pairs={{0,4},{1,5},{2,6},{3,7},{4,0},{5,1},{6,2},{7,3},{8,12},{9,13},{10,... | collective-permute-start | bytes 49160 | tf_op jit(solution)/shard_map/ppermute | solution.py:393
  51.3 3.8 %collective-permute-start.11 = (f32[4,1024]{1,0:T(4,128)S(1)}, f32[4,1024]{1,0:T(4,128)S(1)}, u32[]{:S(2)}, u32[]{:S(2)}) collective-permute-start(f32[4,1024]{1,0:T(4,128)S(1)} %finish_rows.1), channel_id=1, source_target_pairs={{0,8},{8,0},{16,24},{24,16},{1,9},{9,1},{17,25},{25,17},{2,10},{10... | collective-permute-start | bytes 49160 | tf_op jit(solution)/shard_map/ppermute | solution.py:439
  55.1 4.9 %collective-permute-start.12 = (f32[8,1024]{1,0:T(8,128)S(1)}, f32[8,1024]{1,0:T(8,128)S(1)}, u32[]{:S(2)}, u32[]{:S(2)}) collective-permute-start(f32[8,1024]{1,0:T(8,128)S(1)} %pad_maximum_fusion.near_ref), channel_id=1, source_target_pairs={{0,16},{8,24},{16,0},{24,8},{1,17},{9,25},{17,1},{25,9},{2,18},{10... | collective-permute-start | bytes 98312 | tf_op jit(solution)/shard_map/ppermute | solution.py:439
